TPU v7x, 128 devices: a whole 4x4x4 slice. The times are simulated.
128 devices in a mesh: lon: 32 (over z, x, y_hi), lat: 4 (over y_lo, core).
Axes of the slice: x: 4, y: 4 (y_hi: 2, y_lo: 2; y = y_hi * 2 + y_lo), z: 4, core: 2. Of those that a mesh axis runs over, the one named last changes fastest.
Arguments:
- kappa_east: float32 [64, 4096], P('lat', 'lon'), may hold values from 0.02 to 0.2
- kappa_north: float32 [64, 4096], P('lat', 'lon'), may hold values from 0.02 to 0.2
- depth: int32 [64, 4096], P('lat', 'lon'), may hold values from 0 to 75
- sigma: float32 [151], replicated, may hold values from 0.3 to 3
- obs_precision: float32 [151], replicated, may hold values from 0.5 to 4
- obs_tile: int32 [16384, 1], P(('lon', 'lat')), may hold values from 0 to 31; in each aligned block of 128 rows (0 to 127, 128 to 255, ...) at most 8 rows name the same one
- obs_col: int32 [16384], P(('lon', 'lat')), may hold values from 0 to 127
- obs_lat: int32 [16384], P(('lon', 'lat')), may hold values from 0 to 15
- innovation: float32 [151, 16384], P(None, ('lon', 'lat')), may hold values from -6 to 6
Outputs:
- increment: float32 [151, 64, 4096], P(None, 'lat', 'lon')
- residual: float32 [151, 64, 4096], P(None, 'lat', 'lon')
Inputs may be any that keep to these rules, and one draw needn't show every extreme that they name: `obs_tile`: among the 128 profiles listed on one device, no longitude tile is named by more than 8, a bound that some block reaches.
All inputs are finite; a program needn't handle non-finite values.
Results may differ from a plain program's by a relative error of at most 0.00013.
Values sent between devices are 32-bit elements; how exact they have to be, the bound alone decides.
No kernel may reach another device: no remote copies, remote signals or barrier semaphores. Data moves between devices by JAX's collectives and lax.ppermute only.
A program may use at most 128 MiB of HBM per device.

v0:
```python
import jax
import jax.numpy as jnp
from jax import lax
from jax.sharding import PartitionSpec as P

NZ = 75
ITERS = 2


def padded(cells, sides, width):
    for axis, dim in sides:
        count = lax.axis_size(axis)
        head = lax.slice_in_dim(cells, 0, width, axis=dim)
        tail = lax.slice_in_dim(cells, cells.shape[dim] - width, cells.shape[dim], axis=dim)
        cells = jnp.concatenate(
            [
                lax.ppermute(tail, axis, [(i, (i + 1) % count) for i in range(count)]),
                cells,
                lax.ppermute(head, axis, [((i + 1) % count, i) for i in range(count)]),
            ],
            axis=dim,
        )
    return cells


def pass_step(v, face_east, face_north):
    centre = v[:, 1:-1, 1:-1]
    out = centre + face_east[:, 1:-1, 1:-1] * (v[:, 1:-1, 2:] - centre)
    out = out + face_east[:, 1:-1, :-2] * (v[:, 1:-1, :-2] - centre)
    out = out + face_north[:, 1:-1, 1:-1] * (v[:, 2:, 1:-1] - centre)
    return out + face_north[:, :-2, 1:-1] * (v[:, :-2, 1:-1] - centre)


def smooth_five(v, face_east, face_north):
    east_one = face_east[:, 4:-4, 4:-4]
    north_one = face_north[:, 4:-4, 4:-4]
    for step in range(5):
        wide = padded(v, (("lon", 2), ("lat", 1)), 1)
        v = pass_step(wide, east_one, north_one)
    return v


def local(
    kappa_east, kappa_north, depth, sigma, obs_precision, obs_tile, obs_col, obs_lat, innovation
):
    rows, cols = kappa_east.shape
    channels = sigma.shape[0]
    lat_tiles = lax.axis_size("lat")
    lat_here = lax.axis_index("lat")
    lon_here = lax.axis_index("lon")
    row_ids = lax.broadcasted_iota(jnp.int32, (rows, cols), 0)
    wall = jnp.logical_and(lat_here == lat_tiles - 1, row_ids == rows - 1)
    north_kept = jnp.where(wall, jnp.float32(0.0), kappa_north)
    stacked = jnp.stack([kappa_east, north_kept, depth.astype(jnp.float32)])
    extended = padded(stacked, (("lon", 2), ("lat", 1)), 6)
    levels = jnp.arange(channels, dtype=jnp.int32)
    level_of = jnp.where(levels < 2 * NZ, levels % NZ, 0).astype(jnp.float32)
    wet_ext = (extended[2][None, :, :] > level_of[:, None, None]).astype(jnp.float32)
    face_east = extended[0][None, 1:-1, 1:-1] * wet_ext[:, 1:-1, 1:-1] * wet_ext[:, 1:-1, 2:]
    face_north = extended[1][None, 1:-1, 1:-1] * wet_ext[:, 1:-1, 1:-1] * wet_ext[:, 2:, 1:-1]
    wet_tile = wet_ext[:, 6:-6, 6:-6]
    scale = sigma[:, None, None]
    weight = obs_precision[:, None]
    tile_of = obs_tile[:, 0]
    band_tile, band_lat, band_col = (
        lax.all_gather(tile_of, "lon", axis=0, tiled=True),
        lax.all_gather(obs_lat, "lon", axis=0, tiled=True),
        lax.all_gather(obs_col, "lon", axis=0, tiled=True),
    )
    owned = (band_tile == lon_here).astype(jnp.float32)
    column = band_lat * cols + band_col

    def adjoint_obs(w):
        band = lax.all_gather(w, "lon", axis=1, tiled=True)
        cells = (
            jnp.zeros((channels, rows * cols), jnp.float32).at[:, column].add(band * owned[None, :])
        )
        return cells.reshape(channels, rows, cols) * wet_tile

    def squares(v):
        return lax.psum(jnp.sum(v * v), ("lon", "lat"))

    rhs = smooth_five(scale * adjoint_obs(weight * innovation), face_east, face_north)
    increment = jnp.zeros_like(rhs)
    residual = rhs
    direction = rhs
    norm_now = squares(residual)
    for step in range(ITERS):
        hessian_u = scale * smooth_five(direction, face_east, face_north)
        flat = (hessian_u * wet_tile).reshape(channels, rows * cols)
        picked = jnp.take(flat, column, axis=1) * owned[None, :]
        hessian_w = weight * lax.psum_scatter(picked, "lon", scatter_dimension=1, tiled=True)
        image = direction + smooth_five(scale * adjoint_obs(hessian_w), face_east, face_north)
        alpha = norm_now / lax.psum(jnp.sum(direction * image), ("lon", "lat"))
        increment = increment + alpha * direction
        residual = residual - alpha * image
        norm_next = squares(residual)
        direction = residual + norm_next / norm_now * direction
        norm_now = norm_next
    return (increment, residual)


def solution(mesh):
    return jax.shard_map(
        local,
        mesh=mesh,
        in_specs=(
            P("lat", "lon"),
            P("lat", "lon"),
            P("lat", "lon"),
            P(),
            P(),
            P(("lon", "lat"), None),
            P(("lon", "lat")),
            P(("lon", "lat")),
            P(None, ("lon", "lat")),
        ),
        out_specs=(P(None, "lat", "lon"), P(None, "lat", "lon")),
        check_vma=False,
    )
```

profile of v0, /device:TPU:1, one launch (start us, length us, event | category | flops | bytes accessed | tf_op | source)
XLA Modules:
  0.0 1674.6 jit_solution(10457384750685610686)
XLA Ops:
  21.4 76.0 %all-gather = s32[4096,1]{0,1:T(1,128)S(1)} all-gather(s32[128,1]{0,1:T(1,128)} %param.16), channel_id=2, replica_groups=mesh['lon'=32,'lat'=4] {'lon'}, dimensions={0}, use_global_device_ids=true | all-gather | bytes 16896 | tf_op jit(solution)/shard_map/all_gather | solution.py:66
  97.4 73.2 %all-gather.2 = s32[32,1,128]{2,1,0:T(1,128)S(1)} all-gather(s32[1,1,128]{2,1,0:T(1,128)} %bitcast.60), channel_id=1, replica_groups=mesh['lon'=32,'lat'=4] {'lon'}, dimensions={0}, use_global_device_ids=true | all-gather | bytes 16896 | tf_op jit(solution)/shard_map/all_gather | solution.py:68
  170.7 76.0 %all-gather.1 = s32[32,1,128]{2,1,0:T(1,128)S(1)} all-gather(s32[1,1,128]{2,1,0:T(1,128)} %bitcast.61), channel_id=1, replica_groups=mesh['lon'=32,'lat'=4] {'lon'}, dimensions={0}, use_global_device_ids=true | all-gather | bytes 16896 | tf_op jit(solution)/shard_map/all_gather | solution.py:67
  247.5 44.2 %collective-permute-start.2 = (f32[3,6,140]{2,1,0:T(8,128)S(1)}, f32[3,6,140]{2,1,0:T(8,128)S(1)}, u32[]{:S(2)}, u32[]{:S(2)}) collective-permute-start(f32[3,6,140]{2,1,0:T(8,128)S(1)} %get-tuple-element.119), channel_id=1, source_target_pairs={{0,1},{1,2},{2,3},{3,0},{4,5},{5,6},{6,7},{7,4},{8,9},{9,10},{10,1... | collective-permute-start | bytes 30248 | tf_op jit(solution)/shard_map/ppermute | solution.py:17
  298.5 26.5 %scatter_custom_fusion = f32[151,2048]{0,1:T(8,128)} fusion(s32[4096]{0:T(1024)S(1)} %get-tuple-element.124, f32[151,4096]{0,1:T(8,128)} %all-gather.7.cloned.1.call-done, f32[4096]{0:T(1024)S(1)} %bitcast.50, f32[]{:T(128)} %constant.19.clone.1), kind=kCustom, calls=%fused_computation.14 | custom fusion | flops 1236992 | bytes 3727364 | tf_op jit(solution)/shard_map/scatter-add | solution.py:76
  349.9 8.1 collective-permute-start.8
  422.2 8.1 collective-permute-start.24
  439.9 8.1 collective-permute-start.28
  457.8 8.2 collective-permute-start.32
  476.2 8.6 collective-permute-start.36
  495.0 8.4 collective-permute-start.40
  516.9 16.2 gather_fusion
  538.4 171.3 %reduce-scatter.3.cloned.1.call-done = f32[151,128]{0,1:T(8,128)} async-done(((f32[151,4096]{0,1:T(8,128)}), f32[151,128]{0,1:T(8,128)}) %reduce-scatter.3.cloned.1.call-update) | async-done | bytes 77328 | tf_op jit(solution)/shard_map/reduce_scatter | solution.py:92
  711.3 100.2 %all-gather.9.cloned.1.call-done = f32[151,4096]{0,1:T(8,128)} async-done(((f32[151,128]{0,1:T(8,128)}), f32[151,4096]{0,1:T(8,128)}) %all-gather.9.cloned.1.call-update) | async-done | bytes 2474000 | tf_op jit(solution)/shard_map/all_gather | solution.py:74
  811.5 25.6 %scatter_custom_fusion.1 = f32[151,2048]{0,1:T(8,128)S(1)} fusion(s32[4096]{0:T(1024)S(1)} %get-tuple-element.124, f32[151,4096]{0,1:T(8,128)} %all-gather.9.cloned.1.call-done, f32[4096]{0:T(1024)S(1)} %bitcast.52, f32[]{:T(128)} %constant.19.clone.1), kind=kCustom, calls=%fused_computation.11 | custom fusion | flops 1236992 | bytes 3727364 | tf_op jit(solution)/shard_map/scatter-add | solution.py:76
  936.6 66.2 %all-reduce = (f32[]{:T(128)}, f32[]{:T(128)}) all-reduce(f32[]{:T(128)} %get-tuple-element.6, f32[]{:T(128)} %get-tuple-element.5), channel_id=1, replica_groups=mesh['lon'=32,'lat'=4] {'lon','lat'}, use_global_device_ids=true, to_apply=%region_2.3 | all-reduce | flops 2 | bytes 16 | tf_op jit(solution)/shard_map/psum | solution.py:81
  1007.0 62.7 %psum.30 = f32[]{:T(128)} all-reduce(f32[]{:T(128)} %multiply_reduce_fusion.1), channel_id=1, replica_groups=mesh['lon'=32,'lat'=4] {'lon','lat'}, use_global_device_ids=true, to_apply=%region_8.10 | all-reduce | flops 1 | bytes 8 | tf_op jit(solution)/shard_map/psum | solution.py:81
  1130.1 8.1 collective-permute-start.76
  1148.3 8.5 collective-permute-start.80
  1169.7 16.2 gather_fusion.1
  1191.2 171.9 %reduce-scatter.5.cloned.1.call-done = f32[151,128]{0,1:T(8,128)} async-done(((f32[151,4096]{0,1:T(8,128)}), f32[151,128]{0,1:T(8,128)}) %reduce-scatter.5.cloned.1.call-update) | async-done | bytes 77328 | tf_op jit(solution)/shard_map/reduce_scatter | solution.py:92
  1364.7 100.1 %all-gather.11.cloned.1.call-done = f32[151,4096]{0,1:T(8,128)} async-done(((f32[151,128]{0,1:T(8,128)}), f32[151,4096]{0,1:T(8,128)}) %all-gather.11.cloned.1.call-update) | async-done | bytes 2474000 | tf_op jit(solution)/shard_map/all_gather | solution.py:74
  1464.8 25.5 %scatter_custom_fusion.2 = f32[151,2048]{0,1:T(8,128)S(1)} fusion(s32[4096]{0:T(1024)S(1)} %get-tuple-element.124, f32[151,4096]{0,1:T(8,128)} %all-gather.11.cloned.1.call-done, f32[4096]{0:T(1024)S(1)} %bitcast.54, f32[]{:T(128)} %constant.19.clone.1), kind=kCustom, calls=%fused_computation.8 | custom fusion | flops 1236992 | bytes 3727364 | tf_op jit(solution)/shard_map/scatter-add | solution.py:76
  1589.0 66.5 %psum.31 = f32[]{:T(128)} all-reduce(f32[]{:T(128)} %get-tuple-element.9), channel_id=1, replica_groups=mesh['lon'=32,'lat'=4] {'lon','lat'}, use_global_device_ids=true, to_apply=%region_12.14 | all-reduce | flops 1 | bytes 8 | tf_op jit(solution)/shard_map/psum | solution.py:94
  (472 shorter events, 470.0 us)
Async XLA Ops:
  7.2 291.3 %all-gather.7.cloned.1.call-start = ((), (), s32[]{:S(2)}) async-start(), calls=%async_computation.2 | async-start | bytes 4325376 | tf_op jit(solution)/shard_map/all_gather | solution.py:74
  9.6 700.0 %reduce-scatter.3.cloned.1.call-start = ((), (), s32[]{:S(2)}) async-start(), calls=%async_computation.3 | async-start | bytes 4325376 | tf_op jit(solution)/shard_map/reduce_scatter | solution.py:92
  11.9 234.8 %collective-permute-start = (f32[3,16,6]{2,1,0:T(8,128)S(1)}, f32[3,16,6]{2,1,0:T(8,128)S(1)}, u32[]{:S(2)}, u32[]{:S(2)}) collective-permute-start(f32[3,16,6]{2,1,0:T(8,128)S(1)} %get-tuple-element.121), channel_id=1, source_target_pairs={{0,4},{4,8},{8,12},{12,16},{16,20},{20,24},{24,28},{28,32},{32,36}... | collective-permute-start | bytes 3464 | tf_op jit(solution)/shard_map/ppermute | solution.py:17
  15.6 231.1 %collective-permute-start.1 = (f32[3,16,6]{2,1,0:T(8,128)S(1)}, f32[3,16,6]{2,1,0:T(8,128)S(1)}, u32[]{:S(2)}, u32[]{:S(2)}) collective-permute-start(f32[3,16,6]{2,1,0:T(8,128)S(1)} %get-tuple-element.122), channel_id=1, source_target_pairs={{4,0},{8,4},{12,8},{16,12},{20,16},{24,20},{28,24},{32,28},{36,32}... | collective-permute-start | bytes 3464 | tf_op jit(solution)/shard_map/ppermute | solution.py:19
  247.5 45.1 %collective-permute-start.2 = (f32[3,6,140]{2,1,0:T(8,128)S(1)}, f32[3,6,140]{2,1,0:T(8,128)S(1)}, u32[]{:S(2)}, u32[]{:S(2)}) collective-permute-start(f32[3,6,140]{2,1,0:T(8,128)S(1)} %get-tuple-element.119), channel_id=1, source_target_pairs={{0,1},{1,2},{2,3},{3,0},{4,5},{5,6},{6,7},{7,4},{8,9},{9,10},{10,1... | collective-permute-start | bytes 30248 | tf_op jit(solution)/shard_map/ppermute | solution.py:17
  337.5 9.2 collective-permute-start.7
  349.6 9.4 collective-permute-start.9
  422.1 9.3 collective-permute-start.25
  422.2 9.2 collective-permute-start.24
  439.8 9.2 collective-permute-start.29
  457.8 9.4 collective-permute-start.33
  457.8 9.3 collective-permute-start.32
  476.1 9.3 collective-permute-start.37
  476.2 9.5 collective-permute-start.36
  494.9 9.6 collective-permute-start.41
  495.0 9.5 collective-permute-start.40
  538.3 273.2 %all-gather.9.cloned.1.call-start = ((), (), s32[]{:S(2)}) async-start(), calls=%async_computation.4 | async-start | bytes 4325376 | tf_op jit(solution)/shard_map/all_gather | solution.py:74
  711.2 651.9 %reduce-scatter.5.cloned.1.call-start = ((), (), s32[]{:S(2)}) async-start(), calls=%async_computation.5 | async-start | bytes 4325376 | tf_op jit(solution)/shard_map/reduce_scatter | solution.py:92
  1094.7 9.4 collective-permute-start.69
  1112.2 9.2 collective-permute-start.73
  1130.1 9.3 collective-permute-start.77
  1148.2 9.5 collective-permute-start.81
  1148.3 9.4 collective-permute-start.80
  1191.2 273.7 %all-gather.11.cloned.1.call-start = ((), (), s32[]{:S(2)}) async-start(), calls=%async_computation.6 | async-start | bytes 4325376 | tf_op jit(solution)/shard_map/all_gather | solution.py:74
  (107 other events, 1429.7 us)
Sparse Core Ops, SparseCore 0:
  11.7 83.1 all-gather.6
  538.4 171.1 reduce-scatter.2
  713.3 98.1 all-gather.8
  1191.3 171.8 reduce-scatter.4
  1366.7 98.1 all-gather.10
where the time goes:
time: 1680 us; the launch traced here: 1670 us
  waiting for transfers between devices  685 us (41%)
  blocking collectives  421 us (25%)
  starting transfers between devices  288 us (17%)
  other arithmetic  212 us (13%)
  local copies, waits for them, and re-layouts  48.8 us (3%)
  between operations  20.2 us (1%)
    reduce_scatter x2, waiting for transfers between devices, local(): lax.psum_scatter(picked, 'lon', scatter_dimension=1, tiled=True)  343 us
    ppermute x52, starting transfers between devices, padded(): lax.ppermute(head, axis, [((i + 1) % count, i) for i in range(count)])  203 us
    all_gather x3, waiting for transfers between devices, adjoint_obs(): band = lax.all_gather(w, 'lon', axis=1, tiled=True)  200 us
    psum x2, blocking collectives, squares(): return lax.psum(jnp.sum(v * v), ('lon', 'lat'))  129 us
    ppermute x52, starting transfers between devices, padded(): lax.ppermute(tail, axis, [(i, (i + 1) % count) for i in range(count)])  85.3 us
    scatter-add x3, other arithmetic, adjoint_obs(): jnp.zeros((channels, rows * cols), jnp.float32).at[:, column]  77.6 us
    all_gather x1, blocking collectives, local(): lax.all_gather(tile_of, 'lon', axis=0, tiled=True)  76 us
    all_gather x1, blocking collectives, local(): lax.all_gather(obs_lat, 'lon', axis=0, tiled=True)  76 us
  transfers between devices with their start and end apart: 109, of which 80 were waited for; matrix products, arithmetic and copies ran while one was open for 1% of the time, Pallas kernels for 0%

commit v1 on v0

v1 whole, which is shorter than its diff:
```python
import jax
import jax.numpy as jnp
from jax import lax
from jax.experimental import pallas as pl
from jax.experimental.pallas import tpu as pltpu
from jax.sharding import PartitionSpec as P

NZ = 75
CAP = 8
HALF = 76
QUART = 38
SLOT = 40
IDX = 80
PAIRS = 5
KINDS = 15
ROWS = 57
DEPTH = 58
LANES = 128
EDGE = 32
BAND = 16
ALL = ("lon", "lat")
VMEM_LIMIT = 60 * 1024 * 1024


def split_parts(x, count):
    parts = []
    for step in range(count):
        part = x.astype(jnp.bfloat16)
        parts.append(part)
        if step + 1 < count:
            x = x - part.astype(jnp.float32)
    return parts


def pack_kernel(tiles, tile_col, tile_row, obs_lat, obs_col, values, out):
    trow = tile_row[...]
    seen = jnp.logical_and(
        tile_col[...] == trow,
        lax.broadcasted_iota(jnp.int32, (LANES, LANES), 0)
        < lax.broadcasted_iota(jnp.int32, (LANES, LANES), 1),
    )
    rank = jnp.sum(jnp.where(seen, 1.0, 0.0), axis=0, keepdims=True).astype(jnp.int32)
    place = (obs_lat[...] * LANES + obs_col[...] + 1).astype(jnp.float32)
    slots = lax.broadcasted_iota(jnp.int32, (tiles * CAP, LANES), 0)
    marks = []
    for shift in (0, 1, tiles - 1):
        at = lax.rem(trow + shift, tiles) * CAP + rank
        marks.append(jnp.where(slots == at, 1.0, 0.0).astype(jnp.bfloat16))
    lines = lax.broadcasted_iota(jnp.int32, (16, LANES), 0)
    for half in range(2):
        vals = values[half]
        blank = jnp.zeros((IDX, LANES), jnp.float32)
        total = None
        for block in range(3):
            pieces = [vals if j == block else blank for j in range(3)]
            pieces.append(jnp.where(lines == block, place, 0.0))
            right = jnp.concatenate(pieces, axis=0)
            for part in split_parts(right, 3):
                term = lax.dot_general(
                    marks[block],
                    part,
                    (((1,), (1,)), ((), ())),
                    preferred_element_type=jnp.float32,
                )
                total = term if total is None else total + term
        cube = total.reshape(tiles, CAP, 256)
        out[:, half] = cube
        out[:, 2 + half] = cube


def main_kernel(where_ref, recv, geo, par, keep, send, sums, V, FE, FN, DC, XM, XP, G2, LEV):
    y = where_ref[0]
    core = where_ref[1]
    r_low = y * 7
    lane = lax.broadcasted_iota(jnp.int32, (8, LANES), 1)
    l127, l63, l0, l64 = lane == 127, lane == 63, lane == 0, lane == 64
    inner = jnp.logical_and(lane >= 32, lane < 96)

    lane2 = lax.broadcasted_iota(jnp.int32, (64, LANES), 1)
    row2 = lax.broadcasted_iota(jnp.int32, (64, LANES), 0)
    d_own, d_rim = geo[2], geo[5]
    d_turn = pltpu.roll(d_own, 64, 1)
    east_own = jnp.where(lane2 == 127, pltpu.roll(d_rim, 127, 1), pltpu.roll(d_own, 127, 1))
    east_rim = jnp.where(
        lane2 == 127,
        pltpu.roll(d_own, 127, 1),
        jnp.where(lane2 == 63, pltpu.roll(d_turn, 127, 1), pltpu.roll(d_rim, 127, 1)),
    )
    for kind, (ke, kn, d, e) in enumerate(
        ((geo[0], geo[1], d_own, east_own), (None, None, None, None), (geo[3], geo[4], d_rim, east_rim))
    ):
        if kind == 1:
            continue
        wall = jnp.where(row2 == 63, 0.0, kn)
        fields = (ke, jnp.minimum(d, e), wall, jnp.minimum(d, pltpu.roll(d, 63, 0)), d)
        for which, field in enumerate(fields):
            G2[kind * 5 + which] = field
            if kind == 0:
                G2[5 + which] = pltpu.roll(field, 64, 1)
    for p in range(PAIRS):
        low = par[0, pl.ds(8 * p, 8), :]
        high = par[0, pl.ds(8 * (p + 5), 8), :]
        LEV[p * 3] = low
        LEV[p * 3 + 1] = high
        LEV[p * 3 + 2] = jnp.where(inner, high, low)

    lanes_a = lax.broadcasted_iota(jnp.int32, (256, 256), 1)
    lanes_b = lax.broadcasted_iota(jnp.int32, (256, LANES), 1)

    def band(k, carry):
        block = recv[:, k].reshape(256, 256)
        turned = block.T
        places = block[:, 240:243].astype(jnp.int32) - 1
        main_col = jnp.bitwise_and(places[:, 0:1], 127)
        left_col = jnp.bitwise_and(places[:, 1:2], 127)
        right_col = jnp.bitwise_and(places[:, 2:3], 127)
        hot_main = jnp.logical_or(
            lanes_a == main_col, lanes_a == 128 + jnp.bitwise_and(main_col + 64, 127)
        )
        left_ok = left_col >= LANES - EDGE
        hot_left = jnp.logical_and(
            left_ok, jnp.logical_or(lanes_b == left_col, lanes_b == left_col - 64)
        )
        right_ok = right_col < EDGE
        hot_right = jnp.logical_and(
            right_ok, jnp.logical_or(lanes_b == right_col, lanes_b == right_col + 64)
        )
        as16 = lambda m: jnp.where(m, 1.0, 0.0).astype(jnp.bfloat16)
        hot_main, hot_left, hot_right = as16(hot_main), as16(hot_left), as16(hot_right)
        rows_at = lax.shift_right_arithmetic(turned[240:248].astype(jnp.int32) - 1, 7)
        totals = []
        for b, hot in ((0, hot_main), (1, hot_left), (2, hot_right)):
            vals = turned[b * IDX : (b + 1) * IDX]
            at = rows_at[b : b + 1]
            acc = None
            for part in split_parts(vals, 3):
                wide = jnp.concatenate(
                    [part * jnp.where(at == i, 1.0, 0.0).astype(jnp.bfloat16) for i in range(BAND)],
                    axis=0,
                )
                term = jnp.dot(wide, hot, preferred_element_type=jnp.float32)
                acc = term if acc is None else acc + term
            totals.append(acc)
        row0 = k * BAND * IDX
        XM[pl.ds(pl.multiple_of(row0, 8), BAND * IDX), :] = totals[0]
        XP[pl.ds(pl.multiple_of(row0, 8), BAND * IDX), :] = totals[1] + totals[2]
        return carry

    lax.fori_loop(0, recv.shape[1], band, 0)

    def at(kind, row):
        return pl.multiple_of((kind * DEPTH + row) * 8, 8)

    def fill(rho, carry):
        row = rho + r_low
        base = row * IDX

        def tile(ref, t, off):
            return ref[pl.ds(pl.multiple_of(base + 8 * t, 8), 8), off : off + LANES]

        counts = (
            jnp.broadcast_to(tile(XM, 4, 0)[7:8], (8, LANES)),
            jnp.broadcast_to(tile(XM, 9, 128)[7:8], (8, LANES)),
            jnp.broadcast_to(jnp.where(inner, tile(XP, 9, 0), tile(XP, 4, 0))[7:8], (8, LANES)),
        )
        line = [[G2[k * 5 + f, pl.ds(row, 1), :] for f in range(5)] for k in range(3)]
        for p in range(PAIRS):
            raw = (
                tile(XM, p, 0),
                tile(XM, p + 5, 128),
                jnp.where(inner, tile(XP, p + 5, 0), tile(XP, p, 0)),
            )
            w_low, w_high = par[1, pl.ds(8 * p, 8), :], par[1, pl.ds(8 * (p + 5), 8), :]
            s_low, s_high = par[2, pl.ds(8 * p, 8), :], par[2, pl.ds(8 * (p + 5), 8), :]
            w = (w_low, w_high, jnp.where(inner, w_high, w_low))
            s = (s_low, s_high, jnp.where(inner, s_high, s_low))
            for k in range(3):
                lev = LEV[p * 3 + k]
                ke, de, kn, dn, d = line[k]
                where = pl.ds(at(p * 3 + k, rho), 8)
                FE[where, :] = jnp.where(de > lev, ke, 0.0)
                FN[where, :] = jnp.where(dn > lev, kn, 0.0)
                wet = d > lev
                V[where, :] = jnp.where(wet, raw[k] * w[k], 0.0)
                DC[where, :] = jnp.where(wet, counts[k] * s[k], 0.0)
        return carry

    lax.fori_loop(0, ROWS, fill, 0)
    for kind in range(KINDS):
        V[pl.ds((kind * DEPTH + ROWS) * 8, 8), :] = jnp.zeros((8, LANES), jnp.float32)

    def smooth(start, rows):
        def one(step, carry):
            p = lax.rem(step, PAIRS)
            v = [V[pl.ds(at(p * 3 + k, start), 8), :] for k in range(3)]
            gone = [None, None, None]
            for i in range(rows):
                here = [pl.ds(at(p * 3 + k, start + i), 8) for k in range(3)]
                north = [V[pl.ds(at(p * 3 + k, start + i + 1), 8), :] for k in range(3)]
                t = [pltpu.roll(x, 127, 1) for x in v]
                e = (
                    jnp.where(l127, t[2], t[0]),
                    jnp.where(l63, t[2], t[1]),
                    jnp.where(l127, t[0], jnp.where(l63, t[1], t[2])),
                )
                flux = [FE[here[k], :] * (e[k] - v[k]) for k in range(3)]
                u = [pltpu.roll(x, 1, 1) for x in flux]
                west = (
                    jnp.where(l0, u[2], u[0]),
                    jnp.where(l64, u[2], u[1]),
                    jnp.where(l0, u[0], jnp.where(l64, u[1], u[2])),
                )
                rise = [FN[here[k], :] * (north[k] - v[k]) for k in range(3)]
                for k in range(3):
                    out = (v[k] + flux[k]) - west[k] + rise[k]
                    if gone[k] is not None:
                        out = out - gone[k]
                    V[here[k], :] = out
                v, gone = north, rise
            return carry

        lax.fori_loop(0, 5 * PAIRS, one, 0)

    def weigh(start, rows):
        def one(j, carry):
            for kind in range(KINDS):
                here = pl.ds(at(kind, start + j), 8)
                V[here, :] = V[here, :] * DC[here, :]
            return carry

        lax.fori_loop(0, rows, one, 0)

    def store(which):
        for target, tile_row in ((keep, core), (send, 1 - core)):
            low = 25 * y + 16 * tile_row
            for kind in range(2):

                def one(p, carry):
                    for s in range(8):
                        for j in range(2):
                            src = (((p * 3 + kind) * DEPTH) + low + 8 * j) * 8 + s
                            x = V[pl.ds(src, 8, stride=8), :]
                            if kind == 1:
                                x = pltpu.roll(x, 64, 1)
                            target[which, SLOT * kind + 8 * p + s, 8 * j : 8 * j + 8, :] = x
                    return carry

                lax.fori_loop(0, PAIRS, one, 0)

    smooth(y * 0, 57)
    store(0)
    smooth(y * 5, 52)
    weigh(y * 10, 47)
    smooth(y * 10, 47)
    store(1)
    smooth(y * 15, 42)
    weigh(y * 20, 37)
    smooth(y * 20, 37)
    store(2)

    zero = jnp.zeros((8, LANES), jnp.float32)

    def whole(x):
        return jnp.sum(jnp.sum(x, axis=1, keepdims=True), axis=0, keepdims=True)

    def first(i, acc):
        bb, bm = acc
        for ref in (keep, send):
            for j in range(2):
                here = slice(8 * j, 8 * j + 8)
                b, m = ref[0, i, here, :], ref[1, i, here, :]
                bb, bm = bb + b * b, bm + b * m
        return bb, bm

    bb, bm = (whole(x) for x in lax.fori_loop(0, IDX, first, (zero, zero)))
    mu = jnp.where(bb > 0.0, bm / jnp.where(bb > 0.0, bb, 1.0), 0.0)
    mu_all = jnp.broadcast_to(mu, (8, LANES))

    def second(i, acc):
        zz, zy, zm, by, zb = acc
        for ref in (keep, send):
            for j in range(2):
                here = slice(8 * j, 8 * j + 8)
                b, m, n = ref[0, i, here, :], ref[1, i, here, :], ref[2, i, here, :]
                z = m - mu_all * b
                q = n - mu_all * m
                zz, zy, zm = zz + z * z, zy + z * q, zm + z * m
                by, zb = by + b * q, zb + z * b
        return zz, zy, zm, by, zb

    rest = [whole(x) for x in lax.fori_loop(0, IDX, second, (zero,) * 5)]
    lane_row = lax.broadcasted_iota(jnp.int32, (1, LANES), 1)
    packed = jnp.zeros((1, LANES), jnp.float32)
    for j, x in enumerate([bb, bm, mu] + rest):
        packed = jnp.where(lane_row == j, x, packed)
    sums[...] = jnp.broadcast_to(packed, sums.shape)


def last_kernel(where_ref, sums, keep, got, increment, residual):
    core = where_ref[1]
    table = sums[...]

    def col(j):
        return table[:, j : j + 1]

    def total(x):
        return jnp.sum(x, axis=0, keepdims=True)

    bb, bm, mus, zz, zy, zm, by, zb = (col(j) for j in range(8))
    rr = total(bb)
    h = total(bm)
    mu = h / rr
    off = mus - mu
    a1 = rr / (rr + h)
    z_z = total(zz + 2.0 * off * zb + off * off * bb)
    z_m = total(zm + off * bm)
    b_q = total(by + off * bm)
    z_q = total(zy + off * (zm + by) + off * off * bm)
    new = a1 * a1 * z_z
    beta = new / rr
    size = new + beta * beta * rr
    curve = size + a1 * a1 * z_q - a1 * beta * (z_m + b_q) + beta * beta * h
    a2 = new / curve
    spread = lambda x: jnp.broadcast_to(x, (8, LANES))
    mu, a1, a2, beta = spread(mu), spread(a1), spread(a2), spread(beta)

    def write(ref, idx, channel):
        for j in range(2):
            here = slice(8 * j, 8 * j + 8)
            b, m, n = ref[0, idx, here, :], ref[1, idx, here, :], ref[2, idx, here, :]
            r = a1 * (mu * b - m)
            image = a1 * (mu * m - n) + beta * m
            d = r + beta * b
            increment[channel, here, :] = a1 * b + a2 * d
            residual[channel, here, :] = r - a2 * (d + image)

    for ref, half in ((keep, core), (got, 1 - core)):
        for kind in range(2):
            count = QUART if kind == 0 else QUART - half

            def one(i, carry):
                write(ref, SLOT * kind + i, HALF * half + QUART * kind + i)
                return carry

            lax.fori_loop(0, count, one, 0)


def spec(memory_space=pltpu.VMEM):
    return pl.BlockSpec(memory_space=memory_space)


def local(
    kappa_east, kappa_north, depth, sigma, obs_precision, obs_tile, obs_col, obs_lat, innovation
):
    f32 = jnp.float32
    channels = sigma.shape[0]
    lon_tiles = lax.axis_size("lon")
    lat_tiles = lax.axis_size("lat")
    lat_here = lax.axis_index("lat")
    place = jnp.stack([lat_here // 2, lat_here % 2]).astype(jnp.int32)
    core = lat_here % 2

    def halves(x, fill):
        tail = x.shape[1:]
        pad = jnp.zeros((2 * HALF - channels,) + tail, f32)
        ones = jnp.concatenate([jnp.zeros((1,) + tail, f32), jnp.full((1,) + tail, fill, f32)])
        full = jnp.concatenate([x, pad])
        parts = []
        for q in range(4):
            parts += [full[q * QUART : (q + 1) * QUART], ones]
        return jnp.concatenate(parts).reshape((2, IDX) + tail)

    packed = pl.pallas_call(
        lambda *refs: pack_kernel(lon_tiles, *refs),
        out_shape=jax.ShapeDtypeStruct((lon_tiles, lat_tiles, CAP, 256), f32),
        in_specs=[spec()] * 5,
        out_specs=spec(),
        compiler_params=pltpu.CompilerParams(vmem_limit_bytes=VMEM_LIMIT),
        name="pack",
    )(
        obs_tile,
        obs_tile.reshape(1, LANES),
        obs_lat.reshape(1, LANES),
        obs_col.reshape(1, LANES),
        halves(innovation, 1.0),
    )
    recv = lax.all_to_all(
        packed.reshape(lon_tiles * lat_tiles, CAP, 256), ALL, 0, 0, tiled=True
    ).reshape(lon_tiles, lat_tiles, CAP, 256)

    stacked = jnp.stack([kappa_east, kappa_north, depth.astype(f32)])
    count = lon_tiles
    right = lax.ppermute(stacked[:, :, :EDGE], "lon", [((i + 1) % count, i) for i in range(count)])
    left = lax.ppermute(stacked[:, :, -EDGE:], "lon", [(i, (i + 1) % count) for i in range(count)])
    rim = jnp.concatenate([right, left, right, left], axis=2)
    geo = lax.all_gather(jnp.concatenate([stacked, rim]), "lat", axis=1, tiled=True)

    order = jnp.arange(4 * QUART, dtype=jnp.int32)
    level = jnp.where(order < 2 * NZ, order % NZ, 0)
    level = jnp.where(order < channels, level, 1 << 20).astype(f32)
    pads = jnp.zeros((2 * HALF - channels,), f32)
    scale = jnp.concatenate([sigma, pads])
    weight = jnp.concatenate([obs_precision, pads])

    def own(x, fill):
        mine = lax.dynamic_slice_in_dim(x, core * HALF, HALF)
        fills = jnp.full((2,), fill, f32)
        return jnp.concatenate([mine[:QUART], fills, mine[QUART:], fills])

    par = jnp.stack(
        [own(level, float(1 << 20)), own(scale * weight, 0.0), own(scale * scale * weight, 0.0)]
    )
    par = jnp.broadcast_to(par[:, :, None], (3, IDX, LANES))

    tile_shape = jax.ShapeDtypeStruct((3, IDX, BAND, LANES), f32)
    keep, send, sums = pl.pallas_call(
        main_kernel,
        out_shape=(
            tile_shape,
            tile_shape,
            jax.ShapeDtypeStruct((lon_tiles * lat_tiles, LANES), f32),
        ),
        in_specs=[spec(pltpu.SMEM), spec(), spec(), spec()],
        out_specs=(spec(), spec(), spec()),
        scratch_shapes=[
            pltpu.VMEM((KINDS * DEPTH * 8, LANES), f32),
            pltpu.VMEM((KINDS * DEPTH * 8, LANES), f32),
            pltpu.VMEM((KINDS * DEPTH * 8, LANES), f32),
            pltpu.VMEM((KINDS * DEPTH * 8, LANES), f32),
            pltpu.VMEM((64 * IDX, 256), f32),
            pltpu.VMEM((64 * IDX, LANES), f32),
            pltpu.VMEM((KINDS, 64, LANES), f32),
            pltpu.VMEM((KINDS, 8, LANES), f32),
        ],
        compiler_params=pltpu.CompilerParams(vmem_limit_bytes=VMEM_LIMIT),
        name="iterate",
    )(place, recv, geo, par)

    sums = lax.all_to_all(sums, ALL, 0, 0, tiled=True)
    got = lax.ppermute(send, "lat", [(i, i ^ 1) for i in range(lat_tiles)])
    out = jax.ShapeDtypeStruct((channels, BAND, LANES), f32)
    return pl.pallas_call(
        last_kernel,
        out_shape=(out, out),
        in_specs=[spec(pltpu.SMEM), spec(), spec(), spec()],
        out_specs=(spec(), spec()),
        compiler_params=pltpu.CompilerParams(vmem_limit_bytes=VMEM_LIMIT),
        name="combine",
    )(place, sums, keep, got)


def solution(mesh):
    return jax.shard_map(
        local,
        mesh=mesh,
        in_specs=(
            P("lat", "lon"),
            P("lat", "lon"),
            P("lat", "lon"),
            P(),
            P(),
            P(("lon", "lat"), None),
            P(("lon", "lat")),
            P(("lon", "lat")),
            P(None, ("lon", "lat")),
        ),
        out_specs=(P(None, "lat", "lon"), P(None, "lat", "lon")),
        check_vma=False,
    )
```

time: 1680 us -> 345 us (0.21)
  waiting for transfers between devices: 685 us -> 6.62 us
  blocking collectives: 421 us -> 26 us
  Pallas kernels: 0 us -> 276 us
  starting transfers between devices: 288 us -> 20.2 us
  other arithmetic: 212 us -> 2.38 us
  local copies, waits for them, and re-layouts: 48.8 us -> 12.6 us
  between operations: 20.2 us -> 0.73 us
    reduce_scatter x2 -> x0, waiting for transfers between devices: 343 us -> none  [local(): lax.psum_scatter(picked, 'lon', scatter_dimension=1, tiled=True)]
    ppermute x104 -> x3, starting transfers between devices: 288 us -> 10.7 us  [the longest x1 9.42 us: local(): lax.ppermute(stacked[:, :, :EDGE], 'lon', [((i + 1) % count, i) for i in...]
    pallas_call x0 -> x3, Pallas kernels: none -> 276 us  [the longest x1 267 us: local(): pl.pallas_call(main_kernel, out_shape=(tile_shape, tile_shape, jax.ShapeD...]
    all_gather x3 -> x1, blocking collectives: 225 us -> 10.9 us  [local(): lax.all_gather(jnp.concatenate([stacked, rim]), 'lat', axis=1, tiled=True)]
    all_gather x3 -> x0, waiting for transfers between devices: 200 us -> none  [adjoint_obs(): band = lax.all_gather(w, 'lon', axis=1, tiled=True)]
    psum x3 -> x0, blocking collectives: 195 us -> none  [the longest x2 129 us: squares(): return lax.psum(jnp.sum(v * v), ('lon', 'lat'))]
    ppermute x104 -> x3, waiting for transfers between devices: 141 us -> 0.01 us  [the longest x1 0.01 us: local(): got = lax.ppermute(send, 'lat', [(i, i ^ 1) for i in range(lat_tiles)])]
    scatter-add x3 -> x0, other arithmetic: 77.6 us -> none  [adjoint_obs(): jnp.zeros((channels, rows * cols), jnp.float32).at[:, column]]
  transfers between devices with their start and end apart: 109 -> 4, of which waited for: 80 -> 1; matrix products, arithmetic and copies ran while one was open for 1% -> 3% of each run, Pallas kernels for 0% -> 1%
where the time goes in v1:
time: 345 us; the launch traced here: 344 us
  Pallas kernels  276 us (80%)
  blocking collectives  26 us (8%)
  starting transfers between devices  20.2 us (6%)
  local copies, waits for them, and re-layouts  12.6 us (4%)
  waiting for transfers between devices  6.62 us (2%)
    pallas_call x1, Pallas kernels, local(): pl.pallas_call(main_kernel, out_shape=(tile_shape, tile_shape, jax.ShapeD...  267 us
    all_to_all x1, blocking collectives, local(): sums = lax.all_to_all(sums, ALL, 0, 0, tiled=True)  15.2 us
    all_gather x1, blocking collectives, local(): lax.all_gather(jnp.concatenate([stacked, rim]), 'lat', axis=1, tiled=True)  10.9 us
    all_to_all x1, starting transfers between devices, local(): lax.all_to_all(packed.reshape(lon_tiles * lat_tiles, CAP, 256), ALL, 0, 0...  9.56 us
    ppermute x1, starting transfers between devices, local(): lax.ppermute(stacked[:, :, :EDGE], 'lon', [((i + 1) % count, i) for i in...  9.42 us
    concatenate x1, local copies, waits for them, and re-layouts, halves(): return jnp.concatenate(parts).reshape((2, IDX) + tail)  7.61 us
  transfers between devices with their start and end apart: 4, of which 1 were waited for; matrix products, arithmetic and copies ran while one was open for 3% of the time, Pallas kernels for 1%

profile of v1, /device:TPU:1, one launch (start us, length us, event | category | flops | bytes accessed | tf_op | source)
XLA Modules:
  0.0 344.3 jit_solution(5099776124741946399)
XLA Ops:
  0.6 0.7 convert_bitcast_fusion
  1.3 0.7 pad_maximum_fusion
  2.1 9.4 %collective-permute-start = (f32[3,16,32]{2,1,0:T(8,128)S(1)}, f32[3,16,32]{2,1,0:T(8,128)S(1)}, u32[]{:S(2)}, u32[]{:S(2)}) collective-permute-start(f32[3,16,32]{2,1,0:T(8,128)S(1)} %get-tuple-element.12), channel_id=1, source_target_pairs={{4,0},{8,4},{12,8},{16,12},{20,16},{24,20},{28,24},{32,28},{36,32}... | collective-permute-start | bytes 18440 | tf_op jit(solution)/shard_map/ppermute | solution.py:393
  11.6 1.4 copy.12.refs_0_
  13.0 0.8 pad_slice_fusion
  13.8 7.6 %concatenate.29 = f32[160,128]{1,0:T(8,128)} concatenate(f32[38,128]{1,0:T(8,128)S(1)} %get-tuple-element.10, f32[2,128]{1,0:T(2,128)} %constant.51.clone.1, f32[38,128]{1,0:T(8,128)S(1)} %get-tuple-element.9, f32[2,128]{1,0:T(2,128)} %constant.51.clone.1, f32[38,128]{1,0:T(8,128)S(1)} %get-tuple-element.11, f32[2,128]{1,0:T(2,128)} %constant.51.clone.1, ...), dimensions={0} | concatenate | bytes 163840 | tf_op jit(solution)/shard_map/concatenate | solution.py:371
  21.4 2.8 pack.1
  24.2 9.6 %all-to-all-start = ((f32[128,8,256]{2,1,0:T(8,128)}), f32[128,8,256]{2,1,0:T(8,128)S(1)}, u32[]{:S(2)}, u32[]{:S(2)}) async-start(f32[128,8,256]{2,1,0:T(8,128)} %bitcast.23), calls=%async_computation | async-start | bytes 2097152 | tf_op jit(solution)/shard_map/all_to_all | solution.py:387
  33.8 0.1 dynamic_slice.9
  33.9 0.1 fusion.7
  34.0 0.1 dynamic_slice.10
  34.2 0.1 maximum_bitcast_fusion
  34.3 0.1 fusion.5
  34.4 0.6 pad_add_fusion.where_ref
  35.1 0.1 maximum_maximum_fusion
  35.2 10.9 %all_gather.3.geo = f32[6,64,128]{2,1,0:T(8,128)} all-gather(f32[6,16,128]{2,1,0:T(8,128)S(1)} %maximum_maximum_fusion), channel_id=1, replica_groups=mesh['lon'=32,'lat'=4] {'lat'}, dimensions={1}, use_global_device_ids=true | all-gather | bytes 245760 | tf_op jit(solution)/shard_map/all_gather | solution.py:396
  46.0 6.6 %all-to-all-done = f32[128,8,256]{2,1,0:T(8,128)S(1)} async-done(((f32[128,8,256]{2,1,0:T(8,128)}), f32[128,8,256]{2,1,0:T(8,128)S(1)}, u32[]{:S(2)}, u32[]{:S(2)}) %all-to-all-start) | async-done | bytes 1048608 | tf_op jit(solution)/shard_map/all_to_all | solution.py:387
  52.6 0.9 broadcast_in_dim.13.par
  53.5 0.1 copy-done
  53.7 267.4 %iterate.1 = (f32[3,80,16,128]{3,2,1,0:T(8,128)}, f32[3,80,16,128]{3,2,1,0:T(8,128)}, f32[128,128]{1,0:T(8,128)}) custom-call(s32[2]{0:T(128)} %pad_add_fusion.where_ref, f32[32,4,8,256]{3,2,1,0:T(8,128)} %bitcast.22, f32[6,64,128]{2,1,0:T(8,128)} %all_gather.3.geo, f32[3,80,128]{2,1,0:T(8,128)} %broadcast_in_dim.13.par), custom_call_target="tpu_custom_call" | custom-call | tf_op jit(solution)/shard_map/iterate/pallas_call | solution.py:416
  321.0 1.2 collective-permute-start.2
  322.3 15.2 %all_to_all.16 = f32[128,1,128]{2,1,0:T(1,128)} all-to-all(f32[128,1,128]{2,1,0:T(1,128)} %bitcast.26), channel_id=1, replica_groups=mesh['lon'=32,'lat'=4] {'lon','lat'}, dimensions={0} | all-to-all | bytes 131072 | tf_op jit(solution)/shard_map/all_to_all | solution.py:439
  337.4 1.3 copy-done.1
  338.7 5.6 %combine.1 = (f32[151,16,128]{2,1,0:T(8,128)}, f32[151,16,128]{2,1,0:T(8,128)}) custom-call(s32[2]{0:T(128)} %pad_add_fusion.where_ref, f32[128,128]{1,0:T(8,128)} %bitcast.25, f32[3,80,16,128]{3,2,1,0:T(8,128)} %get-tuple-element.6.keep, f32[3,80,16,128]{3,2,1,0:T(8,128)} %copy-done.1), custom_call_target="tpu_custom_call" | custom-call | tf_op jit(solution)/shard_map/combine/pallas_call | solution.py:442
  (22 shorter events, 0.3 us)
Async XLA Ops:
  2.0 31.8 %copy-start.4 = (f32[151]{0:T(256)S(1)}, f32[151]{0:T(256)}, u32[]{:S(2)}) copy-start(f32[151]{0:T(256)} %param.12) | copy-start | bytes 1816
  2.0 31.8 %copy-start.5 = (f32[151]{0:T(256)S(1)}, f32[151]{0:T(256)}, u32[]{:S(2)}) copy-start(f32[151]{0:T(256)} %param.13) | copy-start | bytes 1816
  2.0 33.0 %copy-start.2 = (f32[16,128]{1,0:T(8,128)S(1)}, f32[16,128]{1,0:T(8,128)}, u32[]{:S(2)}) copy-start(f32[16,128]{1,0:T(8,128)} %param.10) | copy-start | bytes 24580
  2.1 33.0 %copy-start.3 = (f32[16,128]{1,0:T(8,128)S(1)}, f32[16,128]{1,0:T(8,128)}, u32[]{:S(2)}) copy-start(f32[16,128]{1,0:T(8,128)} %param.9) | copy-start | bytes 24580
  2.1 32.9 %collective-permute-start = (f32[3,16,32]{2,1,0:T(8,128)S(1)}, f32[3,16,32]{2,1,0:T(8,128)S(1)}, u32[]{:S(2)}, u32[]{:S(2)}) collective-permute-start(f32[3,16,32]{2,1,0:T(8,128)S(1)} %get-tuple-element.12), channel_id=1, source_target_pairs={{4,0},{8,4},{12,8},{16,12},{20,16},{24,20},{28,24},{32,28},{36,32}... | collective-permute-start | bytes 18440 | tf_op jit(solution)/shard_map/ppermute | solution.py:393
  11.6 23.5 %collective-permute-start.1 = (f32[3,16,32]{2,1,0:T(8,128)S(1)}, f32[3,16,32]{2,1,0:T(8,128)S(1)}, u32[]{:S(2)}, u32[]{:S(2)}) collective-permute-start(f32[3,16,32]{2,1,0:T(8,128)S(1)} %get-tuple-element.13), channel_id=1, source_target_pairs={{0,4},{4,8},{8,12},{12,16},{16,20},{20,24},{24,28},{28,32},{32,36}... | collective-permute-start | bytes 18440 | tf_op jit(solution)/shard_map/ppermute | solution.py:394
  24.2 28.5 %all-to-all-start = ((f32[128,8,256]{2,1,0:T(8,128)}), f32[128,8,256]{2,1,0:T(8,128)S(1)}, u32[]{:S(2)}, u32[]{:S(2)}) async-start(f32[128,8,256]{2,1,0:T(8,128)} %bitcast.23), calls=%async_computation | async-start | bytes 2097152 | tf_op jit(solution)/shard_map/all_to_all | solution.py:387
  52.6 1.0 copy-start
  321.0 16.4 %collective-permute-start.2 = (f32[3,80,16,128]{3,2,1,0:T(8,128)}, f32[3,80,16,128]{3,2,1,0:T(8,128)S(1)}, u32[]{:S(2)}, u32[]{:S(2)}) collective-permute-start(f32[3,80,16,128]{3,2,1,0:T(8,128)} %get-tuple-element.7), channel_id=1, source_target_pairs={{0,1},{1,0},{2,3},{3,2},{4,5},{5,4},{6,7},{7,6},{8,9},{9,8},{10,11... | collective-permute-start | bytes 5898248 | tf_op jit(solution)/shard_map/ppermute | solution.py:440
  337.4 1.3 copy-start.1

commit v2 on v0

v2 whole, which is shorter than its diff:
```python
import jax
import jax.numpy as jnp
from jax import lax
from jax.experimental import pallas as pl
from jax.experimental.pallas import tpu as pltpu
from jax.sharding import PartitionSpec as P

NZ = 75
CAP = 8
HALF = 80
GROUPS = 10
SEGS = 12
STEPS = 15
LEFT = 26
ROWS = 64
NEED = 57
LANES = 128
EDGE = 32
BAND = 16
CHUNK = 8
LINE = STEPS * 8
ALL = ("lon", "lat")
VMEM_LIMIT = 60 * 1024 * 1024


def split_parts(x, count):
    parts = []
    for step in range(count):
        part = x.astype(jnp.bfloat16)
        parts.append(part)
        if step + 1 < count:
            x = x - part.astype(jnp.float32)
    return parts


def iota(shape, axis):
    return lax.broadcasted_iota(jnp.int32, shape, axis)


def by_twelve(x):
    return lax.shift_right_logical(x * 5462, 16)


def by_fifteen(x):
    return lax.shift_right_logical(x * 4370, 16)


def as16(mask):
    return jnp.where(mask, 1.0, 0.0).astype(jnp.bfloat16)


def dot(a, b):
    return jnp.dot(a, b, preferred_element_type=jnp.float32)


def dot_nt(a, b):
    return lax.dot_general(a, b, (((1,), (1,)), ((), ())), preferred_element_type=jnp.float32)


def pack_kernel(tiles, tile_col, tile_row, obs_lat, obs_col, values, out, wide):
    channels = values.shape[0]
    wide[144:160, :] = jnp.zeros((16, LANES), jnp.float32)
    wide[0:channels, :] = values[...]
    trow = tile_row[...]
    seen = jnp.logical_and(
        tile_col[...] == trow, iota((LANES, LANES), 0) < iota((LANES, LANES), 1)
    )
    rank = jnp.sum(jnp.where(seen, 1.0, 0.0), axis=0, keepdims=True).astype(jnp.int32)
    slots = iota((tiles * CAP, LANES), 0)
    lines = iota((16, LANES), 0)
    marks, codes = [], []
    for block, (shift, base) in enumerate(((0, LEFT), (1, LEFT - LANES), (tiles - 1, LEFT + LANES))):
        at = lax.rem(trow + shift, tiles) * CAP + rank
        marks.append(as16(slots == at))
        u = obs_col[...] + base
        seg = by_fifteen(jnp.maximum(u, 0))
        good = jnp.logical_and(u >= 0, u < SEGS * STEPS)
        code = jnp.where(good, obs_lat[...] * STEPS + u - seg * STEPS + 1, 0)
        codes.append(
            jnp.where(
                lines == 2 * block,
                code.astype(jnp.float32),
                jnp.where(lines == 2 * block + 1, seg.astype(jnp.float32), 0.0),
            )
        )
    blank = jnp.zeros((HALF, LANES), jnp.float32)
    for half in range(2):
        vals = wide[half * HALF : (half + 1) * HALF, :]
        total = None
        for block in range(3):
            pieces = [vals if j == block else blank for j in range(3)] + [codes[block]]
            for part in split_parts(jnp.concatenate(pieces, axis=0), 3):
                term = dot_nt(marks[block], part)
                total = term if total is None else total + term
        cube = total.reshape(tiles, CAP, 256)
        out[:, half] = cube
        out[:, 2 + half] = cube


def main_kernel(where_ref, recv, geo, par, sb, sm, sn, sums, V, W, FE, FN, DC, CNT, G, EXP):
    y = where_ref[0]
    lane = iota((8, LANES), 1)
    seg8 = jnp.where(lane < GROUPS * SEGS, lane - by_twelve(lane) * SEGS, -1)

    own = [geo[f] for f in range(3)]
    both = [jnp.concatenate([geo[f], geo[3 + f]], axis=1) for f in range(3)]
    wide_lane, wide_row = iota((ROWS, 256), 1), iota((ROWS, 256), 0)
    ke, kn, d = both
    kn = jnp.where(wide_row == ROWS - 1, 0.0, kn)
    east = jnp.where(
        wide_lane == LANES + 2 * EDGE - 1,
        jnp.concatenate([pltpu.roll(own[2], 63, 1)] * 2, axis=1),
        pltpu.roll(d, 255, 1),
    )
    fields = (ke, jnp.minimum(d, east), kn, jnp.minimum(d, pltpu.roll(d, ROWS - 1, 0)), d)
    q_lane, q_row = iota((256, LANES), 1), iota((256, LANES), 0)
    q_col = (q_lane - by_twelve(q_lane) * SEGS) * STEPS - LEFT
    parts = [split_parts(x, 3 if f in (0, 2) else 1) for f, x in enumerate(fields)]
    for j in range(STEPS):
        col = q_col + j
        perm = as16(q_row == jnp.where(col < 0, LANES + 2 * EDGE + col, col))
        for f in range(5):
            total = None
            for part in parts[f]:
                term = dot(part, perm)
                total = term if total is None else total + term
            G[f * STEPS + j] = total

    e_lane = iota((256, LANES), 1)
    e_group, e_row = by_twelve(e_lane), iota((256, LANES), 0)
    for g in range(3):
        for s in range(8):
            hit = jnp.logical_and(e_group < GROUPS, e_row == HALF * g + GROUPS * s + e_group)
            EXP[g, :, s * LANES : (s + 1) * LANES] = as16(hit)
        EXP[g, :, 8 * LANES : 9 * LANES] = as16(e_row == 3 * HALF + 2 * g + 1)

    pick = as16(iota((16, 256), 1) == 3 * HALF + iota((16, 256), 0))
    seg_of = jnp.where(e_lane < GROUPS * SEGS, e_lane - e_group * SEGS, -1).astype(jnp.float32)
    cell = (iota((BAND * STEPS, 256), 0) + 1).astype(jnp.float32)

    def band(k, carry):
        hi, mid = split_parts(recv[:, k].reshape(256, 256), 2)
        codes = dot_nt(pick, hi)
        acc, count = None, None
        for g in range(3):
            left = as16(cell == codes[2 * g : 2 * g + 1])
            full = dot(hi, EXP[g])
            rest = dot(mid, EXP[g, :, 0 : 8 * LANES])
            hot = seg_of == full[:, 8 * LANES :]
            for source in (full, rest):
                right = jnp.concatenate(
                    [
                        jnp.where(hot, source[:, s * LANES : (s + 1) * LANES], 0.0).astype(jnp.bfloat16)
                        for s in range(8)
                    ],
                    axis=1,
                )
                term = dot(left, right)
                acc = term if acc is None else acc + term
            term = dot(left, as16(hot))
            count = term if count is None else count + term
        base = k * (BAND * STEPS)
        for s in range(8):
            V[pl.ds(base * 8 + s, BAND * STEPS, stride=8), :] = acc[:, s * LANES : (s + 1) * LANES]
        CNT[pl.ds(pl.multiple_of(base, 8), BAND * STEPS), :] = count
        return carry

    lax.fori_loop(0, recv.shape[1], band, 0)

    def at(row, j):
        return pl.ds(pl.multiple_of(row * LINE + 8 * j, 8), 8)

    level, w_all, s_all = par[0], par[1], par[2]

    def fill(row, carry):
        for j in range(STEPS):
            ke, de, kn, dn, d = [
                G[f * STEPS + j, pl.ds(row, 1), :] for f in range(5)
            ]
            here = at(row, j)
            FE[here, :] = jnp.where(de > level, ke, 0.0)
            FN[here, :] = jnp.where(dn > level, kn, 0.0)
            wet = d > level
            V[here, :] = jnp.where(wet, V[here, :] * w_all, 0.0)
            DC[here, :] = jnp.where(wet, CNT[pl.ds(row * STEPS + j, 1), :] * s_all, 0.0)
        return carry

    lax.fori_loop(0, ROWS, fill, 0)
    for ref in (V, W):
        ref[ROWS * LINE : (ROWS + 1) * LINE, :] = jnp.zeros((LINE, LANES), jnp.float32)

    def sweep(src, dst, number, weighted=False):
        chunks = lax.div(NEED - number + CHUNK - 1, CHUNK)
        start = y * (ROWS - CHUNK * chunks)

        def one(c, carry):
            v, gone = list(carry[:STEPS]), list(carry[STEPS:])
            base = start + c * CHUNK
            for i in range(CHUNK):
                north = [src[at(base + i + 1, j), :] for j in range(STEPS)]
                flux = [None] * STEPS
                last = STEPS - 1
                flux[last] = FE[at(base + i, last), :] * (pltpu.roll(v[0], LANES - 1, 1) - v[last])
                west = pltpu.roll(flux[last], 1, 1)
                for j in range(last):
                    flux[j] = FE[at(base + i, j), :] * (v[j + 1] - v[j])
                for j in list(range(1, STEPS)) + [0]:
                    rise = FN[at(base + i, j), :] * (north[j] - v[j])
                    out = (v[j] + flux[j]) - (flux[j - 1] if j else west) + (rise - gone[j])
                    if weighted:
                        out = out * DC[at(base + i, j), :]
                    dst[at(base + i, j), :] = out
                    gone[j] = rise
                v = north
            return tuple(v) + tuple(gone)

        zero = jnp.zeros((8, LANES), jnp.float32)
        below = jnp.maximum(start - 1, 0)
        v = tuple(src[at(start, j), :] for j in range(STEPS))
        gone = tuple(
            jnp.where(y > 0, FN[at(below, j), :] * (v[j] - src[at(below, j), :]), zero)
            for j in range(STEPS)
        )
        lax.fori_loop(0, chunks, one, v + gone)

    def smooth(src, dst, stage, weighted=False):
        def twice(step, carry):
            number = 5 * stage + 1 + 2 * step
            sweep(src, dst, number)
            sweep(dst, src, number + 1)
            return carry

        lax.fori_loop(0, 2, twice, 0)
        sweep(src, dst, 5 * stage + 5, weighted)

    def save(src, ref):
        def one(i, carry):
            for j in range(STEPS):
                u = seg8 * STEPS + j
                mine = jnp.logical_and(u >= LEFT, u < LEFT + LANES)
                ref[at(i, j), :] = jnp.where(mine, src[at(y * 32 + i, j), :], 0.0)
            return carry

        lax.fori_loop(0, 32, one, 0)

    smooth(V, W, 0)
    save(W, sb)
    smooth(W, V, 1, True)
    smooth(V, W, 2)
    save(W, sm)
    smooth(W, V, 3, True)
    smooth(V, W, 4)
    save(W, sn)

    zero = jnp.zeros((8, LANES), jnp.float32)

    def whole(x):
        return jnp.sum(jnp.sum(x, axis=0, keepdims=True), axis=1, keepdims=True)

    def first(i, acc):
        bb, bm = acc
        for j in range(STEPS):
            b, m = sb[at(i, j), :], sm[at(i, j), :]
            bb, bm = bb + b * b, bm + b * m
        return bb, bm

    bb, bm = (whole(x) for x in lax.fori_loop(0, 32, first, (zero, zero)))
    mu = jnp.where(bb > 0.0, bm / jnp.where(bb > 0.0, bb, 1.0), 0.0)
    mu_all = jnp.broadcast_to(mu, (8, LANES))

    def second(i, acc):
        zz, zy, zm, by, zb = acc
        for j in range(STEPS):
            b, m, n = sb[at(i, j), :], sm[at(i, j), :], sn[at(i, j), :]
            z = m - mu_all * b
            q = n - mu_all * m
            zz, zy, zm = zz + z * z, zy + z * q, zm + z * m
            by, zb = by + b * q, zb + z * b
        return zz, zy, zm, by, zb

    rest = [whole(x) for x in lax.fori_loop(0, 32, second, (zero,) * 5)]
    lane_row = iota((1, LANES), 1)
    packed = jnp.zeros((1, LANES), jnp.float32)
    for j, x in enumerate([bb, bm, mu] + rest):
        packed = jnp.where(lane_row == j, x, packed)
    sums[...] = jnp.broadcast_to(packed, sums.shape)


def spread_kernel(where_ref, sb, sm, sn, keep, send, T, HI, MID, FLAT):
    core = where_ref[1]
    t_row, t_lane = iota((LANES, LANES), 0), iota((LANES, LANES), 1)
    group = by_twelve(t_row)
    col = (t_row - group * SEGS) * STEPS - LEFT
    for j in range(STEPS + 1):
        for t in range(GROUPS):
            hit = jnp.logical_and(group == t, col + j == t_lane) if j < STEPS else t_row < 0
            T[j * LANES : (j + 1) * LANES, t * LANES : (t + 1) * LANES] = as16(hit)
    for j in (STEPS,):
        HI[:, j * LANES : (j + 1) * LANES] = jnp.zeros((256, LANES), jnp.bfloat16)
        MID[:, j * LANES : (j + 1) * LANES] = jnp.zeros((256, LANES), jnp.bfloat16)
    for which, ref in enumerate((sb, sm, sn)):
        cube = ref.reshape(32, STEPS, 8, LANES)
        for j in range(STEPS):
            hi, mid = split_parts(cube[:, j].reshape(256, LANES), 2)
            HI[:, j * LANES : (j + 1) * LANES] = hi
            MID[:, j * LANES : (j + 1) * LANES] = mid
        for t in range(GROUPS // 2):
            lanes = slice(2 * t * LANES, 2 * (t + 1) * LANES)
            pair = dot(HI[...], T[:, lanes]) + dot(MID[...], T[:, lanes])
            FLAT[2 * t * 256 : (2 * t + 1) * 256, :] = pair[:, :LANES]
            FLAT[(2 * t + 1) * 256 : (2 * t + 2) * 256, :] = pair[:, LANES:]
        for target, rows in ((keep, core), (send, 1 - core)):
            for s in range(8):
                for t in range(GROUPS):
                    for jj in range(2):
                        target[which, GROUPS * s + t, 8 * jj : 8 * jj + 8, :] = FLAT[
                            pl.ds(t * 256 + (rows * BAND + 8 * jj) * 8 + s, 8, stride=8), :
                        ]


def last_kernel(where_ref, sums, keep, got, increment, residual):
    core = where_ref[1]
    table = sums[...]

    def col(j):
        return table[:, j : j + 1]

    def total(x):
        return jnp.sum(x, axis=0, keepdims=True)

    bb, bm, mus, zz, zy, zm, by, zb = (col(j) for j in range(8))
    rr = total(bb)
    h = total(bm)
    mu = h / rr
    off = mus - mu
    a1 = rr / (rr + h)
    z_z = total(zz + 2.0 * off * zb + off * off * bb)
    z_m = total(zm + off * bm)
    b_q = total(by + off * bm)
    z_q = total(zy + off * (zm + by) + off * off * bm)
    new = a1 * a1 * z_z
    beta = new / rr
    size = new + beta * beta * rr
    curve = size + a1 * a1 * z_q - a1 * beta * (z_m + b_q) + beta * beta * h
    a2 = new / curve
    spread = lambda x: jnp.broadcast_to(x, (8, LANES))
    mu, a1, a2, beta = spread(mu), spread(a1), spread(a2), spread(beta)

    def write(ref, idx, channel):
        for j in range(2):
            here = slice(8 * j, 8 * j + 8)
            b, m, n = ref[0, idx, here, :], ref[1, idx, here, :], ref[2, idx, here, :]
            r = a1 * (mu * b - m)
            image = a1 * (mu * m - n) + beta * m
            d = r + beta * b
            increment[channel, here, :] = a1 * b + a2 * d
            residual[channel, here, :] = r - a2 * (d + image)

    for ref, half in ((keep, core), (got, 1 - core)):

        def one(i, carry):
            write(ref, i, HALF * half + i)
            return carry

        lax.fori_loop(0, jnp.where(half == 0, HALF, increment.shape[0] - HALF), one, 0)


def spec(memory_space=pltpu.VMEM):
    return pl.BlockSpec(memory_space=memory_space)


def scratch():
    f32 = jnp.float32
    return [
        pltpu.VMEM(((ROWS + 1) * LINE, LANES), f32),
        pltpu.VMEM(((ROWS + 1) * LINE, LANES), f32),
        pltpu.VMEM((ROWS * LINE, LANES), f32),
        pltpu.VMEM((ROWS * LINE, LANES), f32),
        pltpu.VMEM((ROWS * LINE, LANES), f32),
        pltpu.VMEM((ROWS * STEPS, LANES), f32),
        pltpu.VMEM((5 * STEPS, ROWS, LANES), f32),
        pltpu.VMEM((3, 256, 9 * LANES), jnp.bfloat16),
    ]


def local(
    kappa_east, kappa_north, depth, sigma, obs_precision, obs_tile, obs_col, obs_lat, innovation
):
    f32 = jnp.float32
    channels = sigma.shape[0]
    lon_tiles = lax.axis_size("lon")
    lat_tiles = lax.axis_size("lat")
    lat_here = lax.axis_index("lat")
    place = jnp.stack([lat_here // 2, lat_here % 2]).astype(jnp.int32)
    core = lat_here % 2
    params = pltpu.CompilerParams(vmem_limit_bytes=VMEM_LIMIT)

    packed = pl.pallas_call(
        lambda *refs: pack_kernel(lon_tiles, *refs),
        out_shape=jax.ShapeDtypeStruct((lon_tiles, lat_tiles, CAP, 256), f32),
        in_specs=[spec()] * 5,
        out_specs=spec(),
        scratch_shapes=[pltpu.VMEM((2 * HALF, LANES), f32)],
        compiler_params=params,
        name="pack",
    )(
        obs_tile,
        obs_tile.reshape(1, LANES),
        obs_lat.reshape(1, LANES),
        obs_col.reshape(1, LANES),
        innovation,
    )
    recv = lax.all_to_all(
        packed.reshape(lon_tiles * lat_tiles, CAP, 256), ALL, 0, 0, tiled=True
    ).reshape(lon_tiles, lat_tiles, CAP, 256)

    stacked = jnp.stack([kappa_east, kappa_north, depth.astype(f32)])
    count = lon_tiles
    right = lax.ppermute(stacked[:, :, :EDGE], "lon", [((i + 1) % count, i) for i in range(count)])
    left = lax.ppermute(stacked[:, :, -EDGE:], "lon", [(i, (i + 1) % count) for i in range(count)])
    rim = jnp.concatenate([right, left, right, left], axis=2)
    geo = lax.all_gather(jnp.concatenate([stacked, rim]), "lat", axis=1, tiled=True)

    order = core * HALF + jnp.arange(HALF, dtype=jnp.int32)
    level = jnp.where(order < 2 * NZ, order % NZ, jnp.where(order < channels, 0, 1 << 20))
    pads = jnp.zeros((2 * HALF - channels,), f32)
    scale = lax.dynamic_slice_in_dim(jnp.concatenate([sigma, pads]), core * HALF, HALF)
    weight = lax.dynamic_slice_in_dim(jnp.concatenate([obs_precision, pads]), core * HALF, HALF)
    par = jnp.stack([level.astype(f32), scale * weight, scale * scale * weight])
    par = jnp.repeat(par.reshape(3, 8, GROUPS), SEGS, axis=2)
    fills = jnp.broadcast_to(jnp.array([1 << 20, 0, 0], f32)[:, None, None], (3, 8, 8))
    par = jnp.concatenate([par, fills], axis=2)

    series = jax.ShapeDtypeStruct((32 * LINE, LANES), f32)
    sb, sm, sn, sums = pl.pallas_call(
        main_kernel,
        out_shape=(
            series,
            series,
            series,
            jax.ShapeDtypeStruct((lon_tiles * lat_tiles, LANES), f32),
        ),
        in_specs=[spec(pltpu.SMEM), spec(), spec(), spec()],
        out_specs=(spec(), spec(), spec(), spec()),
        scratch_shapes=scratch(),
        compiler_params=params,
        name="iterate",
    )(place, recv, geo, par)

    sums = lax.all_to_all(sums, ALL, 0, 0, tiled=True)
    tile_shape = jax.ShapeDtypeStruct((3, HALF, BAND, LANES), f32)
    keep, send = pl.pallas_call(
        spread_kernel,
        out_shape=(tile_shape, tile_shape),
        in_specs=[spec(pltpu.SMEM), spec(), spec(), spec()],
        out_specs=(spec(), spec()),
        scratch_shapes=[
            pltpu.VMEM((16 * LANES, GROUPS * LANES), jnp.bfloat16),
            pltpu.VMEM((256, 16 * LANES), jnp.bfloat16),
            pltpu.VMEM((256, 16 * LANES), jnp.bfloat16),
            pltpu.VMEM((GROUPS * 256, LANES), f32),
        ],
        compiler_params=params,
        cost_estimate=pl.CostEstimate(flops=8_000_000_000, bytes_accessed=10_000_000, transcendentals=0),
        name="spread",
    )(place, sb, sm, sn)
    send, sums = lax.optimization_barrier((send, sums))
    got = lax.ppermute(send, "lat", [(i, i ^ 1) for i in range(lat_tiles)])
    out = jax.ShapeDtypeStruct((channels, BAND, LANES), f32)
    return pl.pallas_call(
        last_kernel,
        out_shape=(out, out),
        in_specs=[spec(pltpu.SMEM), spec(), spec(), spec()],
        out_specs=(spec(), spec()),
        compiler_params=params,
        name="combine",
    )(place, sums, keep, got)


def solution(mesh):
    return jax.shard_map(
        local,
        mesh=mesh,
        in_specs=(
            P("lat", "lon"),
            P("lat", "lon"),
            P("lat", "lon"),
            P(),
            P(),
            P(("lon", "lat"), None),
            P(("lon", "lat")),
            P(("lon", "lat")),
            P(None, ("lon", "lat")),
        ),
        out_specs=(P(None, "lat", "lon"), P(None, "lat", "lon")),
        check_vma=False,
    )
```

time: 1680 us -> 120 us (0.07)
  waiting for transfers between devices: 685 us -> 13.6 us
  blocking collectives: 421 us -> 6.81 us
  starting transfers between devices: 288 us -> 24.4 us
  other arithmetic: 212 us -> 1.49 us
  Pallas kernels: 0 us -> 68.7 us
  local copies, waits for them, and re-layouts: 48.8 us -> 4.19 us
  between operations: 20.2 us -> 0.8 us
    reduce_scatter x2 -> x0, waiting for transfers between devices: 343 us -> none  [local(): lax.psum_scatter(picked, 'lon', scatter_dimension=1, tiled=True)]
    ppermute x104 -> x3, starting transfers between devices: 288 us -> 9.22 us  [the longest x1 7.97 us: local(): lax.ppermute(stacked[:, :, :EDGE], 'lon', [((i + 1) % count, i) for i in...]
    all_gather x3 -> x1, blocking collectives: 225 us -> 6.81 us  [local(): lax.all_gather(jnp.concatenate([stacked, rim]), 'lat', axis=1, tiled=True)]
    all_gather x3 -> x0, waiting for transfers between devices: 200 us -> none  [adjoint_obs(): band = lax.all_gather(w, 'lon', axis=1, tiled=True)]
    psum x3 -> x0, blocking collectives: 195 us -> none  [the longest x2 129 us: squares(): return lax.psum(jnp.sum(v * v), ('lon', 'lat'))]
    ppermute x104 -> x3, waiting for transfers between devices: 141 us -> 13.6 us  [the longest x1 9.1 us: local(): lax.ppermute(stacked[:, :, -EDGE:], 'lon', [(i, (i + 1) % count) for i in...]
    scatter-add x3 -> x0, other arithmetic: 77.6 us -> none  [adjoint_obs(): jnp.zeros((channels, rows * cols), jnp.float32).at[:, column]]
    pallas_call x0 -> x4, Pallas kernels: none -> 68.7 us  [the longest x1 46.3 us: local(): pl.pallas_call(main_kernel, out_shape=(series, series, series, jax.ShapeD...]
  transfers between devices with their start and end apart: 109 -> 5, of which waited for: 80 -> 3; matrix products, arithmetic and copies ran while one was open for 1% -> 2% of each run, Pallas kernels for 0% -> 12%
where the time goes in v2:
time: 120 us
  Pallas kernels  68.7 us (57%)
  starting transfers between devices  24.4 us (20%)
  waiting for transfers between devices  13.6 us (11%)
  blocking collectives  6.81 us (6%)
  local copies, waits for them, and re-layouts  4.19 us (3%)
  other arithmetic  1.49 us (1%)
    pallas_call x1, Pallas kernels, local(): pl.pallas_call(main_kernel, out_shape=(series, series, series, jax.ShapeD...  46.3 us
    pallas_call x1, Pallas kernels, local(): pl.pallas_call(spread_kernel, out_shape=(tile_shape, tile_shape), in_spec...  14 us
    all_to_all x1, starting transfers between devices, local(): lax.all_to_all(packed.reshape(lon_tiles * lat_tiles, CAP, 256), ALL, 0, 0...  11.5 us
    ppermute x1, waiting for transfers between devices, local(): lax.ppermute(stacked[:, :, -EDGE:], 'lon', [(i, (i + 1) % count) for i in...  9.1 us
    ppermute x1, starting transfers between devices, local(): lax.ppermute(stacked[:, :, :EDGE], 'lon', [((i + 1) % count, i) for i in...  7.97 us
    all_gather x1, blocking collectives, local(): lax.all_gather(jnp.concatenate([stacked, rim]), 'lat', axis=1, tiled=True)  6.81 us
    pallas_call x1, Pallas kernels, local(): pl.pallas_call(last_kernel, out_shape=(out, out), in_specs=[spec(pltpu.SM...  5.57 us
    ppermute x1, waiting for transfers between devices, local(): got = lax.ppermute(send, 'lat', [(i, i ^ 1) for i in range(lat_tiles)])  3.81 us
  transfers between devices with their start and end apart: 5, of which 3 were waited for; matrix products, arithmetic and copies ran while one was open for 2% of the time, Pallas kernels for 12%

profile of v2, /device:TPU:1, one launch (start us, length us, event | category | flops | bytes accessed | tf_op | source)
XLA Modules:
  0.0 120.0 jit_solution(1416174076505280575)
XLA Ops:
  0.7 1.4 %copy.14.refs_0_ = s32[128,1]{1,0:T(8,128)} copy(s32[128,1]{0,1:T(1,128)} %param.15) | data formatting | bytes 1024 | tf_op args[5]
  2.1 2.8 %pack.1 = f32[32,4,8,256]{3,2,1,0:T(8,128)} custom-call(s32[128,1]{1,0:T(8,128)} %copy.14.refs_0_, s32[1,128]{1,0:T(1,128)} %bitcast.23, s32[1,128]{1,0:T(1,128)} %bitcast.24, s32[1,128]{1,0:T(1,128)} %bitcast.25, f32[151,128]{1,0:T(8,128)} %refs_4_.1), custom_call_target="tpu_custom_call" | custom-call | tf_op jit(solution)/shard_map/pack/pallas_call | solution.py:398
  4.9 11.5 %all-to-all-start = ((f32[128,8,256]{2,1,0:T(8,128)}), f32[128,8,256]{2,1,0:T(8,128)S(1)}, u32[]{:S(2)}, u32[]{:S(2)}) async-start(f32[128,8,256]{2,1,0:T(8,128)} %bitcast.16), calls=%async_computation | async-start | bytes 2097152 | tf_op jit(solution)/shard_map/all_to_all | solution.py:413
  16.4 0.1 fusion.9
  16.5 8.0 %collective-permute-start = (f32[3,16,32]{2,1,0:T(8,128)S(1)}, f32[3,16,32]{2,1,0:T(8,128)S(1)}, u32[]{:S(2)}, u32[]{:S(2)}) collective-permute-start(f32[3,16,32]{2,1,0:T(8,128)S(1)} %get-tuple-element.18), channel_id=1, source_target_pairs={{4,0},{8,4},{12,8},{16,12},{20,16},{24,20},{28,24},{32,28},{36,32}... | collective-permute-start | bytes 18440 | tf_op jit(solution)/shard_map/ppermute | solution.py:419
  24.5 0.1 fusion.8
  24.6 0.1 stack.38
  24.7 0.1 stack.39
  24.8 0.1 broadcast_in_dim.16
  24.9 0.1 reshape.86
  25.1 0.7 pad_maximum_fusion.2.par
  25.8 0.6 pad_add_fusion.where_ref
  26.4 0.7 collective-permute-done
  27.1 9.1 %collective-permute-done.1 = f32[3,16,32]{2,1,0:T(8,128)S(1)} collective-permute-done((f32[3,16,32]{2,1,0:T(8,128)S(1)}, f32[3,16,32]{2,1,0:T(8,128)S(1)}, u32[]{:S(2)}, u32[]{:S(2)}) %collective-permute-start.1) | collective-permute-done | bytes 6176 | tf_op jit(solution)/shard_map/ppermute | solution.py:420
  36.2 0.1 maximum_maximum_fusion
  36.3 6.8 %all_gather.3.geo = f32[6,64,128]{2,1,0:T(8,128)} all-gather(f32[6,16,128]{2,1,0:T(8,128)S(1)} %maximum_maximum_fusion), channel_id=1, replica_groups=mesh['lon'=32,'lat'=4] {'lat'}, dimensions={1}, use_global_device_ids=true | all-gather | bytes 245760 | tf_op jit(solution)/shard_map/all_gather | solution.py:422
  43.1 1.0 copy-done
  44.1 46.3 %iterate.1 = (f32[3840,128]{1,0:T(8,128)}, f32[3840,128]{1,0:T(8,128)}, f32[3840,128]{1,0:T(8,128)}, f32[128,128]{1,0:T(8,128)}) custom-call(s32[2]{0:T(128)} %pad_add_fusion.where_ref, f32[32,4,8,256]{3,2,1,0:T(8,128)} %bitcast.15, f32[6,64,128]{2,1,0:T(8,128)} %all_gather.3.geo, f32[3,8,128]{2,1,0:T(8,128)} %pad_maximum_fusion.2.par), custom_call_target="tpu_custom_call" | custom-call | tf_op jit(solution)/shard_map/iterate/pallas_call | solution.py:435
  90.4 3.7 %all-to-all-start.1 = ((f32[128,1,128]{2,1,0:T(1,128)}), f32[128,1,128]{2,1,0:T(1,128)S(1)}, u32[]{:S(2)}, u32[]{:S(2)}) async-start(f32[128,1,128]{2,1,0:T(1,128)} %bitcast.18), calls=%async_computation.1 | async-start | bytes 131072 | tf_op jit(solution)/shard_map/all_to_all | solution.py:450
  94.1 14.0 %spread.1 = (f32[3,80,16,128]{3,2,1,0:T(8,128)}, f32[3,80,16,128]{3,2,1,0:T(8,128)}) custom-call(s32[2]{0:T(128)} %pad_add_fusion.where_ref, f32[3840,128]{1,0:T(8,128)} %get-tuple-element.10.sb, f32[3840,128]{1,0:T(8,128)} %get-tuple-element.11.sm, f32[3840,128]{1,0:T(8,128)} %get-tuple-element.12.sn), custom_call_target="tpu_custom_call" | custom-call | flops 8000000000 | bytes 10000000 | tf_op jit(solution)/shard_map/spread/pallas_call | solution.py:452
  108.1 1.2 %collective-permute-start.2 = (f32[3,80,16,128]{3,2,1,0:T(8,128)}, f32[3,80,16,128]{3,2,1,0:T(8,128)S(1)}, u32[]{:S(2)}, u32[]{:S(2)}) collective-permute-start(f32[3,80,16,128]{3,2,1,0:T(8,128)} %get-tuple-element.17), channel_id=1, source_target_pairs={{0,1},{1,0},{2,3},{3,2},{4,5},{5,4},{6,7},{7,6},{8,9},{9,8},{10,11... | collective-permute-start | bytes 5898248 | tf_op jit(solution)/shard_map/ppermute | solution.py:468
  109.4 3.8 %collective-permute-done.2.got = f32[3,80,16,128]{3,2,1,0:T(8,128)S(1)} collective-permute-done((f32[3,80,16,128]{3,2,1,0:T(8,128)}, f32[3,80,16,128]{3,2,1,0:T(8,128)S(1)}, u32[]{:S(2)}, u32[]{:S(2)}) %collective-permute-start.2) | collective-permute-done | bytes 1966112 | tf_op jit(solution)/shard_map/ppermute | solution.py:468
  113.2 1.3 %copy-done.1 = f32[3,80,16,128]{3,2,1,0:T(8,128)} copy-done((f32[3,80,16,128]{3,2,1,0:T(8,128)}, f32[3,80,16,128]{3,2,1,0:T(8,128)S(1)}, u32[]{:S(2)}) %copy-start.1) | copy-done | bytes 1966104
  114.5 5.6 %combine.1 = (f32[151,16,128]{2,1,0:T(8,128)}, f32[151,16,128]{2,1,0:T(8,128)}) custom-call(s32[2]{0:T(128)} %pad_add_fusion.where_ref, f32[128,128]{1,0:T(8,128)} %bitcast.17, f32[3,80,16,128]{3,2,1,0:T(8,128)} %get-tuple-element.16.keep, f32[3,80,16,128]{3,2,1,0:T(8,128)} %copy-done.1), custom_call_target="tpu_custom_call" | custom-call | tf_op jit(solution)/shard_map/combine/pallas_call | solution.py:470
  (24 shorter events, 0.1 us)
Async XLA Ops:
  0.6 15.8 %copy-start.5 = (s32[16,128]{1,0:T(8,128)S(1)}, s32[16,128]{1,0:T(8,128)}, u32[]{:S(2)}) copy-start(s32[16,128]{1,0:T(8,128)} %param.12) | copy-start | bytes 24580
  0.6 15.8 %copy-start.3 = (f32[16,128]{1,0:T(8,128)S(1)}, f32[16,128]{1,0:T(8,128)}, u32[]{:S(2)}) copy-start(f32[16,128]{1,0:T(8,128)} %param.11) | copy-start | bytes 24580
  0.7 15.8 %copy-start.4 = (f32[16,128]{1,0:T(8,128)S(1)}, f32[16,128]{1,0:T(8,128)}, u32[]{:S(2)}) copy-start(f32[16,128]{1,0:T(8,128)} %param.10) | copy-start | bytes 24580
  0.7 23.8 %copy-start.7 = (f32[151]{0:T(256)S(1)}, f32[151]{0:T(256)}, u32[]{:S(2)}) copy-start(f32[151]{0:T(256)} %param.14) | copy-start | bytes 1816
  0.7 23.8 %copy-start.6 = (f32[151]{0:T(256)S(1)}, f32[151]{0:T(256)}, u32[]{:S(2)}) copy-start(f32[151]{0:T(256)} %param.13) | copy-start | bytes 1816
  2.1 22.9 %copy-start.8 = (f32[3]{0:T(128)S(1)}, f32[3]{0:T(128)}, u32[]{:S(2)}) copy-start(f32[3]{0:T(128)} %constant.58.clone) | copy-start | bytes 40
  4.9 38.2 %all-to-all-start = ((f32[128,8,256]{2,1,0:T(8,128)}), f32[128,8,256]{2,1,0:T(8,128)S(1)}, u32[]{:S(2)}, u32[]{:S(2)}) async-start(f32[128,8,256]{2,1,0:T(8,128)} %bitcast.16), calls=%async_computation | async-start | bytes 2097152 | tf_op jit(solution)/shard_map/all_to_all | solution.py:413
  16.5 10.6 %collective-permute-start = (f32[3,16,32]{2,1,0:T(8,128)S(1)}, f32[3,16,32]{2,1,0:T(8,128)S(1)}, u32[]{:S(2)}, u32[]{:S(2)}) collective-permute-start(f32[3,16,32]{2,1,0:T(8,128)S(1)} %get-tuple-element.18), channel_id=1, source_target_pairs={{4,0},{8,4},{12,8},{16,12},{20,16},{24,20},{28,24},{32,28},{36,32}... | collective-permute-start | bytes 18440 | tf_op jit(solution)/shard_map/ppermute | solution.py:419
  24.5 11.7 %collective-permute-start.1 = (f32[3,16,32]{2,1,0:T(8,128)S(1)}, f32[3,16,32]{2,1,0:T(8,128)S(1)}, u32[]{:S(2)}, u32[]{:S(2)}) collective-permute-start(f32[3,16,32]{2,1,0:T(8,128)S(1)} %get-tuple-element.19), channel_id=1, source_target_pairs={{0,4},{4,8},{8,12},{12,16},{16,20},{20,24},{24,28},{28,32},{32,36}... | collective-permute-start | bytes 18440 | tf_op jit(solution)/shard_map/ppermute | solution.py:420
  43.1 1.0 copy-start
  90.4 17.7 %all-to-all-start.1 = ((f32[128,1,128]{2,1,0:T(1,128)}), f32[128,1,128]{2,1,0:T(1,128)S(1)}, u32[]{:S(2)}, u32[]{:S(2)}) async-start(f32[128,1,128]{2,1,0:T(1,128)} %bitcast.18), calls=%async_computation.1 | async-start | bytes 131072 | tf_op jit(solution)/shard_map/all_to_all | solution.py:450
  108.1 5.1 %copy-start.2 = (f32[128,1,128]{2,1,0:T(1,128)}, f32[128,1,128]{2,1,0:T(1,128)S(1)}, u32[]{:S(2)}) copy-start(f32[128,1,128]{2,1,0:T(1,128)S(1)} %all-to-all-done.1) | copy-start | bytes 196612
  108.1 5.1 %collective-permute-start.2 = (f32[3,80,16,128]{3,2,1,0:T(8,128)}, f32[3,80,16,128]{3,2,1,0:T(8,128)S(1)}, u32[]{:S(2)}, u32[]{:S(2)}) collective-permute-start(f32[3,80,16,128]{3,2,1,0:T(8,128)} %get-tuple-element.17), channel_id=1, source_target_pairs={{0,1},{1,0},{2,3},{3,2},{4,5},{5,4},{6,7},{7,6},{8,9},{9,8},{10,11... | collective-permute-start | bytes 5898248 | tf_op jit(solution)/shard_map/ppermute | solution.py:468
  113.2 1.3 %copy-start.1 = (f32[3,80,16,128]{3,2,1,0:T(8,128)}, f32[3,80,16,128]{3,2,1,0:T(8,128)S(1)}, u32[]{:S(2)}) copy-start(f32[3,80,16,128]{3,2,1,0:T(8,128)S(1)} %collective-permute-done.2.got) | copy-start | bytes 5898244

commit v3 on v2

--- a/solution.py
+++ b/solution.py
@@ -20,7 +20,8 @@
 CHUNK = 8
 LINE = STEPS * 8
 ALL = ("lon", "lat")
-VMEM_LIMIT = 60 * 1024 * 1024
+MIB = 1024 * 1024
+VMEM_LIMIT = 60 * MIB
 
 
 def split_parts(x, count):
@@ -57,13 +58,14 @@
     return lax.dot_general(a, b, (((1,), (1,)), ((), ())), preferred_element_type=jnp.float32)
 
 
-def pack_kernel(tiles, tile_col, tile_row, obs_lat, obs_col, values, out, wide):
+def pack_kernel(tiles, tile_row, obs_lat, obs_col, values, out, wide):
     channels = values.shape[0]
     wide[144:160, :] = jnp.zeros((16, LANES), jnp.float32)
     wide[0:channels, :] = values[...]
     trow = tile_row[...]
+    every = jnp.broadcast_to(trow, (LANES, LANES))
     seen = jnp.logical_and(
-        tile_col[...] == trow, iota((LANES, LANES), 0) < iota((LANES, LANES), 1)
+        every.T == every, iota((LANES, LANES), 0) < iota((LANES, LANES), 1)
     )
     rank = jnp.sum(jnp.where(seen, 1.0, 0.0), axis=0, keepdims=True).astype(jnp.int32)
     slots = iota((tiles * CAP, LANES), 0)
@@ -97,7 +99,9 @@
         out[:, 2 + half] = cube
 
 
-def main_kernel(where_ref, recv, geo, par, sb, sm, sn, sums, V, W, FE, FN, DC, CNT, G, EXP):
+def main_kernel(
+    where_ref, recv, geo, par, out_b, out_m, out_n, sums, V, W, FE, FN, DC, CNT, G, EXP, sb, sm, sn, done
+):
     y = where_ref[0]
     lane = iota((8, LANES), 1)
     seg8 = jnp.where(lane < GROUPS * SEGS, lane - by_twelve(lane) * SEGS, -1)
@@ -233,136 +237,148 @@
         lax.fori_loop(0, 2, twice, 0)
         sweep(src, dst, 5 * stage + 5, weighted)
 
-    def save(src, ref):
+    zero = jnp.zeros((8, LANES), jnp.float32)
+
+    def mine(j):
+        u = seg8 * STEPS + j
+        return jnp.logical_and(u >= LEFT, u < LEFT + LANES)
+
+    def whole(x):
+        return jnp.sum(jnp.sum(x, axis=0, keepdims=True), axis=1, keepdims=True)
+
+    def save(src, ref, use, count):
         def one(i, carry):
+            acc = list(carry)
             for j in range(STEPS):
-                u = seg8 * STEPS + j
-                mine = jnp.logical_and(u >= LEFT, u < LEFT + LANES)
-                ref[at(i, j), :] = jnp.where(mine, src[at(y * 32 + i, j), :], 0.0)
-            return carry
-
-        lax.fori_loop(0, 32, one, 0)
+                x = jnp.where(mine(j), src[at(y * 32 + i, j), :], 0.0)
+                ref[at(i, j), :] = x
+                if count:
+                    for n, term in enumerate(use(x, at(i, j))):
+                        acc[n * 3 + j % 3] = acc[n * 3 + j % 3] + term
+            return tuple(acc)
+
+        acc = lax.fori_loop(0, 32, one, (zero,) * (3 * count))
+        return [whole(acc[3 * n] + acc[3 * n + 1] + acc[3 * n + 2]) for n in range(count)]
 
     smooth(V, W, 0)
-    save(W, sb)
+    save(W, sb, None, 0)
+    copies = [
+        pltpu.make_async_copy(ref, out, done.at[n])
+        for n, (ref, out) in enumerate(((sb, out_b), (sm, out_m), (sn, out_n)))
+    ]
+    copies[0].start()
     smooth(W, V, 1, True)
     smooth(V, W, 2)
-    save(W, sm)
+
+    def first(m, here):
+        b = sb[here, :]
+        return b * b, b * m
+
+    bb, bm = save(W, sm, first, 2)
+    copies[1].start()
+    mu = jnp.where(bb > 0.0, bm / jnp.where(bb > 0.0, bb, 1.0), 0.0)
     smooth(W, V, 3, True)
     smooth(V, W, 4)
-    save(W, sn)
-
-    zero = jnp.zeros((8, LANES), jnp.float32)
-
-    def whole(x):
-        return jnp.sum(jnp.sum(x, axis=0, keepdims=True), axis=1, keepdims=True)
-
-    def first(i, acc):
-        bb, bm = acc
-        for j in range(STEPS):
-            b, m = sb[at(i, j), :], sm[at(i, j), :]
-            bb, bm = bb + b * b, bm + b * m
-        return bb, bm
-
-    bb, bm = (whole(x) for x in lax.fori_loop(0, 32, first, (zero, zero)))
-    mu = jnp.where(bb > 0.0, bm / jnp.where(bb > 0.0, bb, 1.0), 0.0)
     mu_all = jnp.broadcast_to(mu, (8, LANES))
 
-    def second(i, acc):
-        zz, zy, zm, by, zb = acc
-        for j in range(STEPS):
-            b, m, n = sb[at(i, j), :], sm[at(i, j), :], sn[at(i, j), :]
-            z = m - mu_all * b
-            q = n - mu_all * m
-            zz, zy, zm = zz + z * z, zy + z * q, zm + z * m
-            by, zb = by + b * q, zb + z * b
-        return zz, zy, zm, by, zb
-
-    rest = [whole(x) for x in lax.fori_loop(0, 32, second, (zero,) * 5)]
+    def second(n, here):
+        b, m = sb[here, :], sm[here, :]
+        z = m - mu_all * b
+        q = n - mu_all * m
+        return z * z, z * q, z * m, b * q, z * b
+
+    rest = save(W, sn, second, 5)
+    copies[2].start()
     lane_row = iota((1, LANES), 1)
     packed = jnp.zeros((1, LANES), jnp.float32)
     for j, x in enumerate([bb, bm, mu] + rest):
         packed = jnp.where(lane_row == j, x, packed)
     sums[...] = jnp.broadcast_to(packed, sums.shape)
-
-
-def spread_kernel(where_ref, sb, sm, sn, keep, send, T, HI, MID, FLAT):
+    for copy in copies:
+        copy.wait()
+
+
+def spread_kernel(where_ref, sb, sm, sn, keep, send, T, HI, MID, FLAT, HELD, ready):
     core = where_ref[1]
+    copies = [
+        pltpu.make_async_copy(ref, HELD.at[n], ready.at[n]) for n, ref in enumerate((sb, sm, sn))
+    ]
+    for copy in copies:
+        copy.start()
     t_row, t_lane = iota((LANES, LANES), 0), iota((LANES, LANES), 1)
     group = by_twelve(t_row)
     col = (t_row - group * SEGS) * STEPS - LEFT
-    for j in range(STEPS + 1):
-        for t in range(GROUPS):
-            hit = jnp.logical_and(group == t, col + j == t_lane) if j < STEPS else t_row < 0
-            T[j * LANES : (j + 1) * LANES, t * LANES : (t + 1) * LANES] = as16(hit)
-    for j in (STEPS,):
-        HI[:, j * LANES : (j + 1) * LANES] = jnp.zeros((256, LANES), jnp.bfloat16)
-        MID[:, j * LANES : (j + 1) * LANES] = jnp.zeros((256, LANES), jnp.bfloat16)
-    for which, ref in enumerate((sb, sm, sn)):
-        cube = ref.reshape(32, STEPS, 8, LANES)
+    for t in range(GROUPS):
+        goal = jnp.where(group == t, col, -LANES * STEPS) - t_lane
         for j in range(STEPS):
-            hi, mid = split_parts(cube[:, j].reshape(256, LANES), 2)
+            T[j * LANES : (j + 1) * LANES, t * LANES : (t + 1) * LANES] = as16(goal == -j)
+    for which in range(3):
+        copies[which].wait()
+        cube = HELD.reshape(3, 32, STEPS, 8, LANES)
+        for j in range(STEPS):
+            hi, mid = split_parts(cube[which, :, j].reshape(256, LANES), 2)
             HI[:, j * LANES : (j + 1) * LANES] = hi
             MID[:, j * LANES : (j + 1) * LANES] = mid
         for t in range(GROUPS // 2):
             lanes = slice(2 * t * LANES, 2 * (t + 1) * LANES)
             pair = dot(HI[...], T[:, lanes]) + dot(MID[...], T[:, lanes])
-            FLAT[2 * t * 256 : (2 * t + 1) * 256, :] = pair[:, :LANES]
-            FLAT[(2 * t + 1) * 256 : (2 * t + 2) * 256, :] = pair[:, LANES:]
+            for n in range(2):
+                FLAT[2 * t + n] = pair[:, n * LANES : (n + 1) * LANES]
         for target, rows in ((keep, core), (send, 1 - core)):
             for s in range(8):
                 for t in range(GROUPS):
                     for jj in range(2):
                         target[which, GROUPS * s + t, 8 * jj : 8 * jj + 8, :] = FLAT[
-                            pl.ds(t * 256 + (rows * BAND + 8 * jj) * 8 + s, 8, stride=8), :
+                            t, pl.ds((rows * BAND + 8 * jj) * 8 + s, 8, stride=8), :
                         ]
 
 
-def last_kernel(where_ref, sums, keep, got, increment, residual):
-    core = where_ref[1]
-    table = sums[...]
-
-    def col(j):
-        return table[:, j : j + 1]
-
-    def total(x):
-        return jnp.sum(x, axis=0, keepdims=True)
-
-    bb, bm, mus, zz, zy, zm, by, zb = (col(j) for j in range(8))
-    rr = total(bb)
-    h = total(bm)
-    mu = h / rr
-    off = mus - mu
-    a1 = rr / (rr + h)
-    z_z = total(zz + 2.0 * off * zb + off * off * bb)
-    z_m = total(zm + off * bm)
-    b_q = total(by + off * bm)
-    z_q = total(zy + off * (zm + by) + off * off * bm)
-    new = a1 * a1 * z_z
-    beta = new / rr
-    size = new + beta * beta * rr
-    curve = size + a1 * a1 * z_q - a1 * beta * (z_m + b_q) + beta * beta * h
-    a2 = new / curve
-    spread = lambda x: jnp.broadcast_to(x, (8, LANES))
-    mu, a1, a2, beta = spread(mu), spread(a1), spread(a2), spread(beta)
-
-    def write(ref, idx, channel):
-        for j in range(2):
-            here = slice(8 * j, 8 * j + 8)
-            b, m, n = ref[0, idx, here, :], ref[1, idx, here, :], ref[2, idx, here, :]
-            r = a1 * (mu * b - m)
-            image = a1 * (mu * m - n) + beta * m
-            d = r + beta * b
-            increment[channel, here, :] = a1 * b + a2 * d
-            residual[channel, here, :] = r - a2 * (d + image)
-
-    for ref, half in ((keep, core), (got, 1 - core)):
-
+def last_kernel(where_ref, sums, keep, got, increment, residual, held):
+    half = pl.program_id(0) // 2
+
+    def scalars():
+        table = sums[...].T
+
+        def total(x):
+            return jnp.sum(x, axis=1, keepdims=True)
+
+        bb, bm, mus, zz, zy, zm, by, zb = (table[j : j + 1] for j in range(8))
+        rr = total(bb)
+        h = total(bm)
+        mu = h / rr
+        off = mus - mu
+        a1 = rr / (rr + h)
+        z_z = total(zz + 2.0 * off * zb + off * off * bb)
+        z_m = total(zm + off * bm)
+        b_q = total(by + off * bm)
+        z_q = total(zy + off * (zm + by) + off * off * bm)
+        new = a1 * a1 * z_z
+        beta = new / rr
+        size = new + beta * beta * rr
+        curve = size + a1 * a1 * z_q - a1 * beta * (z_m + b_q) + beta * beta * h
+        for n, x in enumerate((mu, a1, new / curve, beta)):
+            held[n] = jnp.broadcast_to(x, (8, LANES))
+
+    pl.when(pl.program_id(0) == 0)(scalars)
+    mu, a1, a2, beta = (held[n] for n in range(4))
+
+    def write(ref):
         def one(i, carry):
-            write(ref, i, HALF * half + i)
+            for c in range(8):
+                for j in range(2):
+                    at = (i * 8 + c, slice(8 * j, 8 * j + 8))
+                    b, m, n = ref[(0,) + at], ref[(1,) + at], ref[(2,) + at]
+                    r = a1 * (mu * b - m)
+                    image = a1 * (mu * m - n) + beta * m
+                    d = r + beta * b
+                    increment[at] = a1 * b + a2 * d
+                    residual[at] = r - a2 * (d + image)
             return carry
 
-        lax.fori_loop(0, jnp.where(half == 0, HALF, increment.shape[0] - HALF), one, 0)
+        lax.fori_loop(0, HALF // 16, one, 0)
+
+    pl.when(half == where_ref[1])(lambda: write(keep))
+    pl.when(half != where_ref[1])(lambda: write(got))
 
 
 def spec(memory_space=pltpu.VMEM):
@@ -380,6 +396,10 @@
         pltpu.VMEM((ROWS * STEPS, LANES), f32),
         pltpu.VMEM((5 * STEPS, ROWS, LANES), f32),
         pltpu.VMEM((3, 256, 9 * LANES), jnp.bfloat16),
+        pltpu.VMEM((32 * LINE, LANES), f32),
+        pltpu.VMEM((32 * LINE, LANES), f32),
+        pltpu.VMEM((32 * LINE, LANES), f32),
+        pltpu.SemaphoreType.DMA((3,)),
     ]
 
 
@@ -393,31 +413,30 @@
     lat_here = lax.axis_index("lat")
     place = jnp.stack([lat_here // 2, lat_here % 2]).astype(jnp.int32)
     core = lat_here % 2
-    params = pltpu.CompilerParams(vmem_limit_bytes=VMEM_LIMIT)
+    params = lambda size: pltpu.CompilerParams(vmem_limit_bytes=size)
 
     packed = pl.pallas_call(
         lambda *refs: pack_kernel(lon_tiles, *refs),
         out_shape=jax.ShapeDtypeStruct((lon_tiles, lat_tiles, CAP, 256), f32),
-        in_specs=[spec()] * 5,
+        in_specs=[spec()] * 4,
         out_specs=spec(),
         scratch_shapes=[pltpu.VMEM((2 * HALF, LANES), f32)],
-        compiler_params=params,
+        compiler_params=params(10 * MIB),
         name="pack",
     )(
-        obs_tile,
         obs_tile.reshape(1, LANES),
         obs_lat.reshape(1, LANES),
         obs_col.reshape(1, LANES),
         innovation,
     )
-    recv = lax.all_to_all(
-        packed.reshape(lon_tiles * lat_tiles, CAP, 256), ALL, 0, 0, tiled=True
-    ).reshape(lon_tiles, lat_tiles, CAP, 256)
-
     stacked = jnp.stack([kappa_east, kappa_north, depth.astype(f32)])
     count = lon_tiles
     right = lax.ppermute(stacked[:, :, :EDGE], "lon", [((i + 1) % count, i) for i in range(count)])
     left = lax.ppermute(stacked[:, :, -EDGE:], "lon", [(i, (i + 1) % count) for i in range(count)])
+    recv = lax.all_to_all(
+        packed.reshape(lon_tiles * lat_tiles, CAP, 256), ALL, 0, 0, tiled=True
+    ).reshape(lon_tiles, lat_tiles, CAP, 256)
+
     rim = jnp.concatenate([right, left, right, left], axis=2)
     geo = lax.all_gather(jnp.concatenate([stacked, rim]), "lat", axis=1, tiled=True)
 
@@ -441,9 +460,9 @@
             jax.ShapeDtypeStruct((lon_tiles * lat_tiles, LANES), f32),
         ),
         in_specs=[spec(pltpu.SMEM), spec(), spec(), spec()],
-        out_specs=(spec(), spec(), spec(), spec()),
+        out_specs=(spec(pltpu.HBM), spec(pltpu.HBM), spec(pltpu.HBM), spec()),
         scratch_shapes=scratch(),
-        compiler_params=params,
+        compiler_params=params(VMEM_LIMIT),
         name="iterate",
     )(place, recv, geo, par)
 
@@ -452,27 +471,44 @@
     keep, send = pl.pallas_call(
         spread_kernel,
         out_shape=(tile_shape, tile_shape),
-        in_specs=[spec(pltpu.SMEM), spec(), spec(), spec()],
+        in_specs=[spec(pltpu.SMEM)] + [spec(pltpu.HBM)] * 3,
         out_specs=(spec(), spec()),
         scratch_shapes=[
-            pltpu.VMEM((16 * LANES, GROUPS * LANES), jnp.bfloat16),
-            pltpu.VMEM((256, 16 * LANES), jnp.bfloat16),
-            pltpu.VMEM((256, 16 * LANES), jnp.bfloat16),
-            pltpu.VMEM((GROUPS * 256, LANES), f32),
+            pltpu.VMEM((STEPS * LANES, GROUPS * LANES), jnp.bfloat16),
+            pltpu.VMEM((256, STEPS * LANES), jnp.bfloat16),
+            pltpu.VMEM((256, STEPS * LANES), jnp.bfloat16),
+            pltpu.VMEM((GROUPS, 256, LANES), f32),
+            pltpu.VMEM((3, 32 * LINE, LANES), f32),
+            pltpu.SemaphoreType.DMA((3,)),
         ],
-        compiler_params=params,
+        compiler_params=params(VMEM_LIMIT),
         cost_estimate=pl.CostEstimate(flops=8_000_000_000, bytes_accessed=10_000_000, transcendentals=0),
         name="spread",
     )(place, sb, sm, sn)
     send, sums = lax.optimization_barrier((send, sums))
     got = lax.ppermute(send, "lat", [(i, i ^ 1) for i in range(lat_tiles)])
     out = jax.ShapeDtypeStruct((channels, BAND, LANES), f32)
+    early = lambda i: jnp.minimum(i, 1)
+    late = lambda i: jnp.maximum(i - 2, 0)
+    block = (3, HALF // 2, BAND, LANES)
     return pl.pallas_call(
         last_kernel,
         out_shape=(out, out),
-        in_specs=[spec(pltpu.SMEM), spec(), spec(), spec()],
-        out_specs=(spec(), spec()),
-        compiler_params=params,
+        grid_spec=pltpu.PrefetchScalarGridSpec(
+            num_scalar_prefetch=1,
+            grid=(4,),
+            in_specs=[
+                pl.BlockSpec((lon_tiles * lat_tiles, LANES), lambda i, w: (0, 0)),
+                pl.BlockSpec(block, lambda i, w: (0, jnp.where(w[1] == 0, early(i), late(i)), 0, 0)),
+                pl.BlockSpec(block, lambda i, w: (0, jnp.where(w[1] == 0, late(i), early(i)), 0, 0)),
+            ],
+            out_specs=(
+                pl.BlockSpec((HALF // 2, BAND, LANES), lambda i, w: (i, 0, 0)),
+                pl.BlockSpec((HALF // 2, BAND, LANES), lambda i, w: (i, 0, 0)),
+            ),
+            scratch_shapes=[pltpu.VMEM((4, 8, LANES), f32)],
+        ),
+        compiler_params=params(16 * MIB),
         name="combine",
     )(place, sums, keep, got)
 

time: 120 us -> 118 us (0.983)
  Pallas kernels: 68.7 us -> 64.6 us
  local copies, waits for them, and re-layouts: 4.19 us -> 5.92 us
    pallas_call x1, Pallas kernels: 5.57 us -> 3.57 us  [local(): pl.pallas_call(last_kernel, out_shape=(out, out), grid_spec=pltpu.Prefetc...]
    unnamed x19 -> x26, local copies, waits for them, and re-layouts: 3.68 us -> 5.41 us
    pallas_call x1, Pallas kernels: 46.3 us -> 44.7 us  [local(): pl.pallas_call(main_kernel, out_shape=(series, series, series, jax.ShapeD...]
where the time goes in v3:
time: 118 us
  Pallas kernels  64.6 us (55%)
  starting transfers between devices  24.5 us (21%)
  waiting for transfers between devices  13.6 us (12%)
  blocking collectives  6.81 us (6%)
  local copies, waits for them, and re-layouts  5.92 us (5%)
  other arithmetic  1.52 us (1%)
    pallas_call x1, Pallas kernels, local(): pl.pallas_call(main_kernel, out_shape=(series, series, series, jax.ShapeD...  44.7 us
    pallas_call x1, Pallas kernels, local(): pl.pallas_call(spread_kernel, out_shape=(tile_shape, tile_shape), in_spec...  14.5 us
    all_to_all x1, starting transfers between devices, local(): lax.all_to_all(packed.reshape(lon_tiles * lat_tiles, CAP, 256), ALL, 0, 0...  11.5 us
    ppermute x1, waiting for transfers between devices, local(): lax.ppermute(stacked[:, :, -EDGE:], 'lon', [(i, (i + 1) % count) for i in...  9.1 us
    ppermute x1, starting transfers between devices, local(): lax.ppermute(stacked[:, :, :EDGE], 'lon', [((i + 1) % count, i) for i in...  7.97 us
    all_gather x1, blocking collectives, local(): lax.all_gather(jnp.concatenate([stacked, rim]), 'lat', axis=1, tiled=True)  6.81 us
    unnamed x26, local copies, waits for them, and re-layouts  5.41 us
    ppermute x1, waiting for transfers between devices, local(): got = lax.ppermute(send, 'lat', [(i, i ^ 1) for i in range(lat_tiles)])  3.81 us
  transfers between devices with their start and end apart: 5, of which 3 were waited for; matrix products, arithmetic and copies ran while one was open for 2% of the time, Pallas kernels for 12%

profile of v3, /device:TPU:1, one launch (start us, length us, event | category | flops | bytes accessed | tf_op | source)
XLA Modules:
  0.0 117.7 jit_solution(17466418598485488814)
XLA Ops:
  0.7 0.9 copy-done.1
  1.6 0.7 copy-done.3
  2.2 0.7 copy-done.4
  2.9 0.7 copy-done.5
  3.5 1.8 %pack.1 = f32[32,4,8,256]{3,2,1,0:T(8,128)} custom-call(s32[1,128]{1,0:T(1,128)S(1)} %bitcast.16, s32[1,128]{1,0:T(1,128)S(1)} %bitcast.17, s32[1,128]{1,0:T(1,128)S(1)} %bitcast.18, f32[151,128]{1,0:T(8,128)S(1)} %copy-done.1), custom_call_target="tpu_custom_call" | custom-call | tf_op jit(solution)/shard_map/pack/pallas_call | solution.py:418
  5.4 11.5 %all-to-all-start = ((f32[128,8,256]{2,1,0:T(8,128)}), f32[128,8,256]{2,1,0:T(8,128)S(1)}, u32[]{:S(2)}, u32[]{:S(2)}) async-start(f32[128,8,256]{2,1,0:T(8,128)} %bitcast.5), calls=%async_computation | async-start | bytes 2097152 | tf_op jit(solution)/shard_map/all_to_all | solution.py:436
  17.0 8.0 %collective-permute-start = (f32[3,16,32]{2,1,0:T(8,128)S(1)}, f32[3,16,32]{2,1,0:T(8,128)S(1)}, u32[]{:S(2)}, u32[]{:S(2)}) collective-permute-start(f32[3,16,32]{2,1,0:T(8,128)S(1)} %get-tuple-element.18), channel_id=1, source_target_pairs={{4,0},{8,4},{12,8},{16,12},{20,16},{24,20},{28,24},{32,28},{36,32}... | collective-permute-start | bytes 18440 | tf_op jit(solution)/shard_map/ppermute | solution.py:434
  25.0 0.1 fusion.8
  25.3 0.1 broadcast_in_dim.16
  25.4 0.1 reshape.86
  25.6 0.7 pad_maximum_fusion.2.par
  26.3 0.7 pad_add_fusion.where_ref
  26.9 0.7 collective-permute-done
  27.6 9.1 %collective-permute-done.1 = f32[3,16,32]{2,1,0:T(8,128)S(1)} collective-permute-done((f32[3,16,32]{2,1,0:T(8,128)S(1)}, f32[3,16,32]{2,1,0:T(8,128)S(1)}, u32[]{:S(2)}, u32[]{:S(2)}) %collective-permute-start.1) | collective-permute-done | bytes 6176 | tf_op jit(solution)/shard_map/ppermute | solution.py:435
  36.7 0.1 maximum_maximum_fusion
  36.8 6.8 %all_gather.3.geo = f32[6,64,128]{2,1,0:T(8,128)} all-gather(f32[6,16,128]{2,1,0:T(8,128)S(1)} %maximum_maximum_fusion), channel_id=1, replica_groups=mesh['lon'=32,'lat'=4] {'lat'}, dimensions={1}, use_global_device_ids=true | all-gather | bytes 245760 | tf_op jit(solution)/shard_map/all_gather | solution.py:441
  43.6 1.0 copy-done.6
  44.6 44.7 %iterate.1 = (f32[3840,128]{1,0:T(8,128)}, f32[3840,128]{1,0:T(8,128)}, f32[3840,128]{1,0:T(8,128)}, f32[128,128]{1,0:T(8,128)}) custom-call(s32[2]{0:T(128)} %pad_add_fusion.where_ref, f32[32,4,8,256]{3,2,1,0:T(8,128)} %bitcast.19, f32[6,64,128]{2,1,0:T(8,128)} %all_gather.3.geo, f32[3,8,128]{2,1,0:T(8,128)} %pad_maximum_fusion.2.par), custom_call_target="tpu_custom_call" | custom-call | tf_op jit(solution)/shard_map/iterate/pallas_call | solution.py:454
  89.2 3.7 %all-to-all-start.1 = ((f32[128,1,128]{2,1,0:T(1,128)}), f32[128,1,128]{2,1,0:T(1,128)S(1)}, u32[]{:S(2)}, u32[]{:S(2)}) async-start(f32[128,1,128]{2,1,0:T(1,128)} %bitcast.20), calls=%async_computation.1 | async-start | bytes 131072 | tf_op jit(solution)/shard_map/all_to_all | solution.py:469
  93.0 14.5 %spread.1 = (f32[3,80,16,128]{3,2,1,0:T(8,128)}, f32[3,80,16,128]{3,2,1,0:T(8,128)}) custom-call(s32[2]{0:T(128)} %pad_add_fusion.where_ref, f32[3840,128]{1,0:T(8,128)} %get-tuple-element.10.sb, f32[3840,128]{1,0:T(8,128)} %get-tuple-element.11.sm, f32[3840,128]{1,0:T(8,128)} %get-tuple-element.12.sn), custom_call_target="tpu_custom_call" | custom-call | flops 8000000000 | bytes 10000000 | tf_op jit(solution)/shard_map/spread/pallas_call | solution.py:471
  107.5 1.3 %collective-permute-start.2 = (f32[3,80,16,128]{3,2,1,0:T(8,128)}, f32[3,80,16,128]{3,2,1,0:T(8,128)S(1)}, u32[]{:S(2)}, u32[]{:S(2)}) collective-permute-start(f32[3,80,16,128]{3,2,1,0:T(8,128)} %get-tuple-element.17), channel_id=1, source_target_pairs={{0,1},{1,0},{2,3},{3,2},{4,5},{5,4},{6,7},{7,6},{8,9},{9,8},{10,11... | collective-permute-start | bytes 5898248 | tf_op jit(solution)/shard_map/ppermute | solution.py:489
  108.8 3.8 %collective-permute-done.2.got = f32[3,80,16,128]{3,2,1,0:T(8,128)S(1)} collective-permute-done((f32[3,80,16,128]{3,2,1,0:T(8,128)}, f32[3,80,16,128]{3,2,1,0:T(8,128)S(1)}, u32[]{:S(2)}, u32[]{:S(2)}) %collective-permute-start.2) | collective-permute-done | bytes 1966112 | tf_op jit(solution)/shard_map/ppermute | solution.py:489
  112.6 1.5 %copy-done = f32[3,80,16,128]{3,2,1,0:T(8,128)S(1)} copy-done((f32[3,80,16,128]{3,2,1,0:T(8,128)S(1)}, f32[3,80,16,128]{3,2,1,0:T(8,128)}, u32[]{:S(2)}) %copy-start) | copy-done | bytes 1966104
  114.2 3.6 %combine.1 = (f32[151,16,128]{2,1,0:T(8,128)}, f32[151,16,128]{2,1,0:T(8,128)}) custom-call(s32[2]{0:T(128)S(1)} %copy-done.2, f32[128,128]{1,0:T(8,128)S(1)} %bitcast.15, f32[3,80,16,128]{3,2,1,0:T(8,128)S(1)} %copy-done, f32[3,80,16,128]{3,2,1,0:T(8,128)S(1)} %collective-permute-done.2.got), custom_call_target="tpu_custom_call" | custom-call | tf_op jit(solution)/shard_map/combine/pallas_call | solution.py:494
  (31 shorter events, 0.4 us)
Async XLA Ops:
  0.6 24.9 %copy-start.12 = (f32[3]{0:T(128)S(1)}, f32[3]{0:T(128)}, u32[]{:S(2)}) copy-start(f32[3]{0:T(128)} %constant.58.clone) | copy-start | bytes 40
  0.6 24.3 %copy-start.11 = (f32[151]{0:T(256)S(1)}, f32[151]{0:T(256)}, u32[]{:S(2)}) copy-start(f32[151]{0:T(256)} %param.14) | copy-start | bytes 1816
  0.7 24.3 %copy-start.10 = (f32[151]{0:T(256)S(1)}, f32[151]{0:T(256)}, u32[]{:S(2)}) copy-start(f32[151]{0:T(256)} %param.13) | copy-start | bytes 1816
  0.7 0.9 copy-start.1
  1.6 0.7 copy-start.3
  2.2 0.7 copy-start.4
  2.9 0.7 copy-start.5
  3.5 13.3 %copy-start.9 = (s32[16,128]{1,0:T(8,128)S(1)}, s32[16,128]{1,0:T(8,128)}, u32[]{:S(2)}) copy-start(s32[16,128]{1,0:T(8,128)} %param.12) | copy-start | bytes 24580
  3.5 13.4 %copy-start.7 = (f32[16,128]{1,0:T(8,128)S(1)}, f32[16,128]{1,0:T(8,128)}, u32[]{:S(2)}) copy-start(f32[16,128]{1,0:T(8,128)} %param.11) | copy-start | bytes 24580
  3.5 13.4 %copy-start.8 = (f32[16,128]{1,0:T(8,128)S(1)}, f32[16,128]{1,0:T(8,128)}, u32[]{:S(2)}) copy-start(f32[16,128]{1,0:T(8,128)} %param.10) | copy-start | bytes 24580
  5.4 38.2 %all-to-all-start = ((f32[128,8,256]{2,1,0:T(8,128)}), f32[128,8,256]{2,1,0:T(8,128)S(1)}, u32[]{:S(2)}, u32[]{:S(2)}) async-start(f32[128,8,256]{2,1,0:T(8,128)} %bitcast.5), calls=%async_computation | async-start | bytes 2097152 | tf_op jit(solution)/shard_map/all_to_all | solution.py:436
  17.0 10.6 %collective-permute-start = (f32[3,16,32]{2,1,0:T(8,128)S(1)}, f32[3,16,32]{2,1,0:T(8,128)S(1)}, u32[]{:S(2)}, u32[]{:S(2)}) collective-permute-start(f32[3,16,32]{2,1,0:T(8,128)S(1)} %get-tuple-element.18), channel_id=1, source_target_pairs={{4,0},{8,4},{12,8},{16,12},{20,16},{24,20},{28,24},{32,28},{36,32}... | collective-permute-start | bytes 18440 | tf_op jit(solution)/shard_map/ppermute | solution.py:434
  25.0 11.7 %collective-permute-start.1 = (f32[3,16,32]{2,1,0:T(8,128)S(1)}, f32[3,16,32]{2,1,0:T(8,128)S(1)}, u32[]{:S(2)}, u32[]{:S(2)}) collective-permute-start(f32[3,16,32]{2,1,0:T(8,128)S(1)} %get-tuple-element.19), channel_id=1, source_target_pairs={{0,4},{4,8},{8,12},{12,16},{16,20},{20,24},{24,28},{28,32},{32,36}... | collective-permute-start | bytes 18440 | tf_op jit(solution)/shard_map/ppermute | solution.py:435
  43.6 1.0 copy-start.6
  89.2 18.2 %all-to-all-start.1 = ((f32[128,1,128]{2,1,0:T(1,128)}), f32[128,1,128]{2,1,0:T(1,128)S(1)}, u32[]{:S(2)}, u32[]{:S(2)}) async-start(f32[128,1,128]{2,1,0:T(1,128)} %bitcast.20), calls=%async_computation.1 | async-start | bytes 131072 | tf_op jit(solution)/shard_map/all_to_all | solution.py:469
  93.0 19.7 %copy-start.2 = (s32[2]{0:T(128)S(1)}, s32[2]{0:T(128)}, u32[]{:S(2)}) copy-start(s32[2]{0:T(128)} %pad_add_fusion.where_ref) | copy-start | bytes 28
  107.5 5.1 %collective-permute-start.2 = (f32[3,80,16,128]{3,2,1,0:T(8,128)}, f32[3,80,16,128]{3,2,1,0:T(8,128)S(1)}, u32[]{:S(2)}, u32[]{:S(2)}) collective-permute-start(f32[3,80,16,128]{3,2,1,0:T(8,128)} %get-tuple-element.17), channel_id=1, source_target_pairs={{0,1},{1,0},{2,3},{3,2},{4,5},{5,4},{6,7},{7,6},{8,9},{9,8},{10,11... | collective-permute-start | bytes 5898248 | tf_op jit(solution)/shard_map/ppermute | solution.py:489
  112.6 1.5 %copy-start = (f32[3,80,16,128]{3,2,1,0:T(8,128)S(1)}, f32[3,80,16,128]{3,2,1,0:T(8,128)}, u32[]{:S(2)}) copy-start(f32[3,80,16,128]{3,2,1,0:T(8,128)} %get-tuple-element.16.keep) | copy-start | bytes 5898244

commit v4 on v3

--- a/solution.py
+++ b/solution.py
@@ -421,7 +421,7 @@
         in_specs=[spec()] * 4,
         out_specs=spec(),
         scratch_shapes=[pltpu.VMEM((2 * HALF, LANES), f32)],
-        compiler_params=params(10 * MIB),
+        compiler_params=params(VMEM_LIMIT),
         name="pack",
     )(
         obs_tile.reshape(1, LANES),

time: 118 us -> 116 us (0.983)
  local copies, waits for them, and re-layouts: 5.92 us -> 3.06 us
    unnamed x26 -> x18, local copies, waits for them, and re-layouts: 5.41 us -> 2.55 us
where the time goes in v4:
time: 116 us
  Pallas kernels  65.5 us (56%)
  starting transfers between devices  24.5 us (21%)
  waiting for transfers between devices  13.6 us (12%)
  blocking collectives  6.81 us (6%)
  local copies, waits for them, and re-layouts  3.06 us (3%)
  other arithmetic  1.49 us (1%)
    pallas_call x1, Pallas kernels, local(): pl.pallas_call(main_kernel, out_shape=(series, series, series, jax.ShapeD...  44.7 us
    pallas_call x1, Pallas kernels, local(): pl.pallas_call(spread_kernel, out_shape=(tile_shape, tile_shape), in_spec...  14.5 us
    all_to_all x1, starting transfers between devices, local(): lax.all_to_all(packed.reshape(lon_tiles * lat_tiles, CAP, 256), ALL, 0, 0...  11.5 us
    ppermute x1, waiting for transfers between devices, local(): lax.ppermute(stacked[:, :, -EDGE:], 'lon', [(i, (i + 1) % count) for i in...  9.1 us
    ppermute x1, starting transfers between devices, local(): lax.ppermute(stacked[:, :, :EDGE], 'lon', [((i + 1) % count, i) for i in...  7.97 us
    all_gather x1, blocking collectives, local(): lax.all_gather(jnp.concatenate([stacked, rim]), 'lat', axis=1, tiled=True)  6.81 us
    ppermute x1, waiting for transfers between devices, local(): got = lax.ppermute(send, 'lat', [(i, i ^ 1) for i in range(lat_tiles)])  3.81 us
    all_to_all x1, starting transfers between devices, local(): sums = lax.all_to_all(sums, ALL, 0, 0, tiled=True)  3.72 us
  transfers between devices with their start and end apart: 5, of which 3 were waited for; matrix products, arithmetic and copies ran while one was open for 2% of the time, Pallas kernels for 12%

profile of v4, /device:TPU:1, one launch (start us, length us, event | category | flops | bytes accessed | tf_op | source)
XLA Modules:
  0.0 115.9 jit_solution(12929440942828528719)
XLA Ops:
  0.7 2.8 %pack.1 = f32[32,4,8,256]{3,2,1,0:T(8,128)} custom-call(s32[1,128]{1,0:T(1,128)} %bitcast.23, s32[1,128]{1,0:T(1,128)} %bitcast.24, s32[1,128]{1,0:T(1,128)} %bitcast.25, f32[151,128]{1,0:T(8,128)} %refs_3_.1), custom_call_target="tpu_custom_call" | custom-call | tf_op jit(solution)/shard_map/pack/pallas_call | solution.py:418
  3.5 11.5 %all-to-all-start = ((f32[128,8,256]{2,1,0:T(8,128)}), f32[128,8,256]{2,1,0:T(8,128)S(1)}, u32[]{:S(2)}, u32[]{:S(2)}) async-start(f32[128,8,256]{2,1,0:T(8,128)} %bitcast.17), calls=%async_computation | async-start | bytes 2097152 | tf_op jit(solution)/shard_map/all_to_all | solution.py:436
  15.1 0.1 fusion.9
  15.1 8.0 %collective-permute-start = (f32[3,16,32]{2,1,0:T(8,128)S(1)}, f32[3,16,32]{2,1,0:T(8,128)S(1)}, u32[]{:S(2)}, u32[]{:S(2)}) collective-permute-start(f32[3,16,32]{2,1,0:T(8,128)S(1)} %get-tuple-element.18), channel_id=1, source_target_pairs={{4,0},{8,4},{12,8},{16,12},{20,16},{24,20},{28,24},{32,28},{36,32}... | collective-permute-start | bytes 18440 | tf_op jit(solution)/shard_map/ppermute | solution.py:434
  23.1 0.1 fusion.8
  23.2 0.1 stack.38
  23.3 0.1 stack.39
  23.4 0.1 broadcast_in_dim.16
  23.5 0.1 reshape.86
  23.6 0.1 broadcast_in_dim.17
  23.7 0.7 pad_maximum_fusion.2.par
  24.4 0.6 pad_add_fusion.where_ref
  25.0 0.7 collective-permute-done
  25.7 9.1 %collective-permute-done.1 = f32[3,16,32]{2,1,0:T(8,128)S(1)} collective-permute-done((f32[3,16,32]{2,1,0:T(8,128)S(1)}, f32[3,16,32]{2,1,0:T(8,128)S(1)}, u32[]{:S(2)}, u32[]{:S(2)}) %collective-permute-start.1) | collective-permute-done | bytes 6176 | tf_op jit(solution)/shard_map/ppermute | solution.py:435
  34.8 0.1 maximum_maximum_fusion
  34.9 6.8 %all_gather.3.geo = f32[6,64,128]{2,1,0:T(8,128)} all-gather(f32[6,16,128]{2,1,0:T(8,128)S(1)} %maximum_maximum_fusion), channel_id=1, replica_groups=mesh['lon'=32,'lat'=4] {'lat'}, dimensions={1}, use_global_device_ids=true | all-gather | bytes 245760 | tf_op jit(solution)/shard_map/all_gather | solution.py:441
  41.7 1.0 copy-done.2
  42.7 44.7 %iterate.1 = (f32[3840,128]{1,0:T(8,128)}, f32[3840,128]{1,0:T(8,128)}, f32[3840,128]{1,0:T(8,128)}, f32[128,128]{1,0:T(8,128)}) custom-call(s32[2]{0:T(128)} %pad_add_fusion.where_ref, f32[32,4,8,256]{3,2,1,0:T(8,128)} %bitcast.16, f32[6,64,128]{2,1,0:T(8,128)} %all_gather.3.geo, f32[3,8,128]{2,1,0:T(8,128)} %pad_maximum_fusion.2.par), custom_call_target="tpu_custom_call" | custom-call | tf_op jit(solution)/shard_map/iterate/pallas_call | solution.py:454
  87.4 3.7 %all-to-all-start.1 = ((f32[128,1,128]{2,1,0:T(1,128)}), f32[128,1,128]{2,1,0:T(1,128)S(1)}, u32[]{:S(2)}, u32[]{:S(2)}) async-start(f32[128,1,128]{2,1,0:T(1,128)} %bitcast.18), calls=%async_computation.1 | async-start | bytes 131072 | tf_op jit(solution)/shard_map/all_to_all | solution.py:469
  91.1 14.5 %spread.1 = (f32[3,80,16,128]{3,2,1,0:T(8,128)}, f32[3,80,16,128]{3,2,1,0:T(8,128)}) custom-call(s32[2]{0:T(128)} %pad_add_fusion.where_ref, f32[3840,128]{1,0:T(8,128)} %get-tuple-element.10.sb, f32[3840,128]{1,0:T(8,128)} %get-tuple-element.11.sm, f32[3840,128]{1,0:T(8,128)} %get-tuple-element.12.sn), custom_call_target="tpu_custom_call" | custom-call | flops 8000000000 | bytes 10000000 | tf_op jit(solution)/shard_map/spread/pallas_call | solution.py:471
  105.6 1.3 %collective-permute-start.2 = (f32[3,80,16,128]{3,2,1,0:T(8,128)}, f32[3,80,16,128]{3,2,1,0:T(8,128)S(1)}, u32[]{:S(2)}, u32[]{:S(2)}) collective-permute-start(f32[3,80,16,128]{3,2,1,0:T(8,128)} %get-tuple-element.17), channel_id=1, source_target_pairs={{0,1},{1,0},{2,3},{3,2},{4,5},{5,4},{6,7},{7,6},{8,9},{9,8},{10,11... | collective-permute-start | bytes 5898248 | tf_op jit(solution)/shard_map/ppermute | solution.py:489
  106.9 3.8 %collective-permute-done.2.got = f32[3,80,16,128]{3,2,1,0:T(8,128)S(1)} collective-permute-done((f32[3,80,16,128]{3,2,1,0:T(8,128)}, f32[3,80,16,128]{3,2,1,0:T(8,128)S(1)}, u32[]{:S(2)}, u32[]{:S(2)}) %collective-permute-start.2) | collective-permute-done | bytes 1966112 | tf_op jit(solution)/shard_map/ppermute | solution.py:489
  110.7 1.5 %copy-done = f32[3,80,16,128]{3,2,1,0:T(8,128)S(1)} copy-done((f32[3,80,16,128]{3,2,1,0:T(8,128)S(1)}, f32[3,80,16,128]{3,2,1,0:T(8,128)}, u32[]{:S(2)}) %copy-start) | copy-done | bytes 1966104
  112.3 3.6 %combine.1 = (f32[151,16,128]{2,1,0:T(8,128)}, f32[151,16,128]{2,1,0:T(8,128)}) custom-call(s32[2]{0:T(128)S(1)} %copy-done.1, f32[128,128]{1,0:T(8,128)S(1)} %bitcast.15, f32[3,80,16,128]{3,2,1,0:T(8,128)S(1)} %copy-done, f32[3,80,16,128]{3,2,1,0:T(8,128)S(1)} %collective-permute-done.2.got), custom_call_target="tpu_custom_call" | custom-call | tf_op jit(solution)/shard_map/combine/pallas_call | solution.py:494
  (23 shorter events, 0.1 us)
Async XLA Ops:
  0.6 23.0 %copy-start.8 = (f32[3]{0:T(128)S(1)}, f32[3]{0:T(128)}, u32[]{:S(2)}) copy-start(f32[3]{0:T(128)} %constant.58.clone) | copy-start | bytes 40
  0.6 14.4 %copy-start.5 = (s32[16,128]{1,0:T(8,128)S(1)}, s32[16,128]{1,0:T(8,128)}, u32[]{:S(2)}) copy-start(s32[16,128]{1,0:T(8,128)} %param.12) | copy-start | bytes 24580
  0.7 14.4 %copy-start.3 = (f32[16,128]{1,0:T(8,128)S(1)}, f32[16,128]{1,0:T(8,128)}, u32[]{:S(2)}) copy-start(f32[16,128]{1,0:T(8,128)} %param.11) | copy-start | bytes 24580
  0.7 14.4 %copy-start.4 = (f32[16,128]{1,0:T(8,128)S(1)}, f32[16,128]{1,0:T(8,128)}, u32[]{:S(2)}) copy-start(f32[16,128]{1,0:T(8,128)} %param.10) | copy-start | bytes 24580
  0.7 22.4 %copy-start.7 = (f32[151]{0:T(256)S(1)}, f32[151]{0:T(256)}, u32[]{:S(2)}) copy-start(f32[151]{0:T(256)} %param.14) | copy-start | bytes 1816
  0.7 22.4 %copy-start.6 = (f32[151]{0:T(256)S(1)}, f32[151]{0:T(256)}, u32[]{:S(2)}) copy-start(f32[151]{0:T(256)} %param.13) | copy-start | bytes 1816
  3.5 38.2 %all-to-all-start = ((f32[128,8,256]{2,1,0:T(8,128)}), f32[128,8,256]{2,1,0:T(8,128)S(1)}, u32[]{:S(2)}, u32[]{:S(2)}) async-start(f32[128,8,256]{2,1,0:T(8,128)} %bitcast.17), calls=%async_computation | async-start | bytes 2097152 | tf_op jit(solution)/shard_map/all_to_all | solution.py:436
  15.1 10.6 %collective-permute-start = (f32[3,16,32]{2,1,0:T(8,128)S(1)}, f32[3,16,32]{2,1,0:T(8,128)S(1)}, u32[]{:S(2)}, u32[]{:S(2)}) collective-permute-start(f32[3,16,32]{2,1,0:T(8,128)S(1)} %get-tuple-element.18), channel_id=1, source_target_pairs={{4,0},{8,4},{12,8},{16,12},{20,16},{24,20},{28,24},{32,28},{36,32}... | collective-permute-start | bytes 18440 | tf_op jit(solution)/shard_map/ppermute | solution.py:434
  23.1 11.7 %collective-permute-start.1 = (f32[3,16,32]{2,1,0:T(8,128)S(1)}, f32[3,16,32]{2,1,0:T(8,128)S(1)}, u32[]{:S(2)}, u32[]{:S(2)}) collective-permute-start(f32[3,16,32]{2,1,0:T(8,128)S(1)} %get-tuple-element.19), channel_id=1, source_target_pairs={{0,4},{4,8},{8,12},{12,16},{16,20},{20,24},{24,28},{28,32},{32,36}... | collective-permute-start | bytes 18440 | tf_op jit(solution)/shard_map/ppermute | solution.py:435
  41.7 1.0 copy-start.2
  87.4 18.2 %all-to-all-start.1 = ((f32[128,1,128]{2,1,0:T(1,128)}), f32[128,1,128]{2,1,0:T(1,128)S(1)}, u32[]{:S(2)}, u32[]{:S(2)}) async-start(f32[128,1,128]{2,1,0:T(1,128)} %bitcast.18), calls=%async_computation.1 | async-start | bytes 131072 | tf_op jit(solution)/shard_map/all_to_all | solution.py:469
  91.1 19.7 %copy-start.1 = (s32[2]{0:T(128)S(1)}, s32[2]{0:T(128)}, u32[]{:S(2)}) copy-start(s32[2]{0:T(128)} %pad_add_fusion.where_ref) | copy-start | bytes 28
  105.6 5.1 %collective-permute-start.2 = (f32[3,80,16,128]{3,2,1,0:T(8,128)}, f32[3,80,16,128]{3,2,1,0:T(8,128)S(1)}, u32[]{:S(2)}, u32[]{:S(2)}) collective-permute-start(f32[3,80,16,128]{3,2,1,0:T(8,128)} %get-tuple-element.17), channel_id=1, source_target_pairs={{0,1},{1,0},{2,3},{3,2},{4,5},{5,4},{6,7},{7,6},{8,9},{9,8},{10,11... | collective-permute-start | bytes 5898248 | tf_op jit(solution)/shard_map/ppermute | solution.py:489
  110.7 1.5 %copy-start = (f32[3,80,16,128]{3,2,1,0:T(8,128)S(1)}, f32[3,80,16,128]{3,2,1,0:T(8,128)}, u32[]{:S(2)}) copy-start(f32[3,80,16,128]{3,2,1,0:T(8,128)} %get-tuple-element.16.keep) | copy-start | bytes 5898244
